TPU v7x, 32 devices: a whole 2x2x4 slice. The times are simulated.
32 devices in a mesh: replica: 2 (over x), section: 4 (over y, core), shard: 4 (over z).
Axes of the slice: x: 2, y: 2, z: 4, core: 2. Of those that a mesh axis runs over, the one named last changes fastest.
Arguments:
- inputs: bfloat16 [2, 1, 128, 1024], P('replica', None, None, 'shard'), may hold values from -17 to 17
- targets: bfloat16 [2, 1, 128, 1024], P('replica', None, None, 'shard'), may hold values from -6 to 6
- weight_a: bfloat16 [2, 4, 1024, 3072], P('replica', 'section', None, 'shard'), may hold values from -6 to 6
- weight_b: bfloat16 [2, 4, 3072, 1024], P('replica', 'section', 'shard'), may hold values from -6 to 6
- moment_a: bfloat16 [2, 4, 1024, 3072], P('replica', 'section', None, 'shard'), may hold values from -3 to 3
- moment_b: bfloat16 [2, 4, 3072, 1024], P('replica', 'section', 'shard'), may hold values from -3 to 3
- routes: int32 [1, 3, 2, 2], replicated, may hold values from 0 to 1, each once within a row
- partners: int32 [4, 2, 2, 2], replicated, may hold values from 0 to 1, as said below
Outputs:
- new_weight_a: bfloat16 [2, 4, 1024, 3072], P('replica', 'section', None, 'shard')
- new_weight_b: bfloat16 [2, 4, 3072, 1024], P('replica', 'section', 'shard')
- new_moment_a: bfloat16 [2, 4, 1024, 3072], P('replica', 'section', None, 'shard')
- new_moment_b: bfloat16 [2, 4, 3072, 1024], P('replica', 'section', 'shard')
Inputs may be any that keep to these rules, and one draw needn't show every extreme that they name: Each routes[m, s, q, :] names every replica once, so each replica of section s + 1 receives exactly one block from every replica of section s. For each section s, projection t and piece k, partners[s, t, k, :] is its own inverse (the partner of the partner is the replica itself); for each s, t and replica r, partners[s, t, :, r] names every replica once, and exactly one piece pairs r with itself.
All inputs are finite; a program needn't handle non-finite values.
Results may differ from a plain program's by a relative error of at most 0.022.
Values may be sent and summed in bfloat16 or wider, within the bound.
No kernel may reach another device: no remote copies, remote signals or barrier semaphores. Data moves between devices by JAX's collectives and lax.ppermute only.
A program may use at most 128 MiB of HBM per device.

v0:
```python
import functools
import math

import jax
import jax.numpy as jnp
from jax import lax
from jax.experimental import pallas as pl
from jax.experimental.pallas import tpu as pltpu
from jax.sharding import PartitionSpec as P

epsilon = 1e-05
inner_rate = 0.5
momentum_decay = 0.9
outer_rate = 0.7

axes = ("replica", "section", "shard")
contract_rows = (((0,), (0,)), ((), ()))
contract_last = (((1,), (1,)), ((), ()))


def norm_scale(rows):
    wide = rows.astype(jnp.float32)
    return lax.rsqrt(jnp.mean(wide * wide, axis=1, keepdims=True) + epsilon)


def dot(left, right, dims=(((1,), (0,)), ((), ()))):
    return lax.dot_general(left, right, dims, preferred_element_type=jnp.float32)


def outer_mix(weight, moment, delta):
    new_moment = momentum_decay * moment + delta
    new_weight = weight - outer_rate * (momentum_decay * new_moment + delta)
    return new_weight.astype(jnp.bfloat16), new_moment.astype(jnp.bfloat16)


def slope_of(preact):
    gate = jax.nn.sigmoid(preact)
    return gate * (1.0 + preact * (1.0 - gate))


def from_panels(array, rows):
    count = array.shape[0] // rows
    return jnp.concatenate([array[i * rows : (i + 1) * rows] for i in range(count)], axis=1)


def pack_kernel(heights, panel, starts, *refs):
    sources, (packed, buffer, read_sems, write_sems) = refs[:-4], refs[-4:]
    reads, writes = [], []
    place = 0
    for i, (source, height) in enumerate(zip(sources, heights)):
        rows = pl.ds(pl.multiple_of(starts[0, i], height), height)
        for column in range(0, source.shape[1], panel):
            k = len(reads)
            there = pl.ds(place, height)
            reads.append(
                pltpu.make_async_copy(
                    source.at[rows, pl.ds(column, panel)], buffer.at[there], read_sems.at[k]
                )
            )
            writes.append(
                pltpu.make_async_copy(buffer.at[there], packed.at[there], write_sems.at[k])
            )
            place += height
    for copy in reads:
        copy.start()
    for read, write in zip(reads, writes):
        read.wait()
        write.start()
    for copy in writes:
        copy.wait()


def pack(arrays, heights, starts, panel):
    counts = [array.shape[1] // panel for array in arrays]
    total = sum(count * height for count, height in zip(counts, heights))
    anywhere = pl.BlockSpec(memory_space=pl.ANY)
    return pl.pallas_call(
        functools.partial(pack_kernel, heights, panel),
        out_shape=jax.ShapeDtypeStruct((total, panel), arrays[0].dtype),
        in_specs=[pl.BlockSpec(memory_space=pltpu.SMEM)] + [anywhere] * len(arrays),
        out_specs=anywhere,
        scratch_shapes=[
            pltpu.VMEM((total, panel), arrays[0].dtype),
            pltpu.SemaphoreType.DMA((sum(counts),)),
            pltpu.SemaphoreType.DMA((sum(counts),)),
        ],
        compiler_params=pltpu.CompilerParams(vmem_limit_bytes=16 * 1024 * 1024),
        cost_estimate=pl.CostEstimate(
            flops=0, bytes_accessed=4 * total * panel, transcendentals=0
        ),
    )(starts, *arrays)


class Sizes:
    def __init__(self, shards, sections, row_count, width, local_hidden, panel, blocks):
        self.shards, self.sections, self.row_count = shards, sections, row_count
        self.width, self.local_hidden, self.panel = width, local_hidden, panel
        self.blocks = blocks
        self.block_rows = row_count // blocks
        self.panels_in = local_hidden // panel
        self.panels_out = width // panel
        self.half = width * self.panels_in
        self.scale_in = 1.0 / math.sqrt(width)
        self.scale_out = 1.0 / math.sqrt(local_hidden * shards)


def chain_kernel(sz, step, forward, backward, holder, *refs):
    refs = list(refs)
    table = refs.pop(0)
    first = forward and step == 0
    received = [] if first else [refs.pop(0) for _ in range(sz.blocks)]
    payloads = [refs.pop(0) for _ in range(sz.shards)]
    del refs[: 2 + (not backward or not forward)]
    if forward and not backward:
        state_in = None
    sends = [refs.pop(0) for _ in range(sz.blocks)]
    rows_hbm = refs.pop(0)
    second_hbm = refs.pop(0)
    slope_hbm = refs.pop(0) if not (forward and backward) else None
    weights, rows, up, out, slope, weight_sems, edge_sems, block_sems, state_sems = refs
    panel, width, hidden_size = sz.panel, sz.width, sz.local_hidden

    def weight_copy(d, which):
        return pltpu.make_async_copy(
            payloads[d].at[pl.ds(which * sz.half, sz.half)],
            weights.at[d, which],
            weight_sems.at[d, which],
        )

    def edge_copy(target, d):
        column = (holder ^ d) * panel
        return pltpu.make_async_copy(
            payloads[d].at[pl.ds(2 * sz.half, sz.row_count)],
            target.at[:, pl.ds(column, panel)],
            edge_sems.at[d],
        )

    def place(line, e):
        return pl.ds(pl.multiple_of(table[line, e], sz.block_rows), sz.block_rows)

    links = sz.sections - 1

    @pl.when(table[links + 1, step] == 1)
    def _():
        arrive = links if forward else step
        leave = links if backward else step
        block_copies = [
            pltpu.make_async_copy(
                received[e], (rows if forward else up).at[place(arrive, e)], block_sems.at[e]
            )
            for e in range(len(received))
        ]
        edge_copies = []
        if first:
            edge_copies = [edge_copy(rows, d) for d in range(sz.shards)]
        elif forward and backward:
            edge_copies = [edge_copy(out, d) for d in range(sz.shards)]
        state_copies = []
        if backward and not forward:
            state_copies = [
                pltpu.make_async_copy(rows_hbm, rows, state_sems.at[0]),
                pltpu.make_async_copy(slope_hbm, slope, state_sems.at[1]),
            ]
        for copy in block_copies + edge_copies + state_copies:
            copy.start()
        order = (0, 1) if forward else (1, 0)
        for d in range(sz.shards):
            for which in order:
                weight_copy(d, which).start()
        for copy in block_copies + edge_copies + state_copies:
            copy.wait()

        wide = rows[...].astype(jnp.float32)
        inverse_rms = lax.rsqrt(jnp.mean(wide * wide, axis=1, keepdims=True) + epsilon)
        store_copies = []
        if forward:
            store_copies.append(pltpu.make_async_copy(rows, rows_hbm, state_sems.at[0]))
            store_copies[-1].start()
            normed = (wide * inverse_rms).astype(jnp.bfloat16)
            total = [jnp.zeros((sz.row_count, panel), jnp.float32) for _ in range(sz.panels_out)]
            for d in range(sz.shards):
                weight_copy(d, 0).wait()
                hidden = []
                for p in range(sz.panels_in):
                    weight = weights[d, 0, p * width : (p + 1) * width, :]
                    preact = dot(normed, weight) * sz.scale_in
                    gate = jax.nn.sigmoid(preact)
                    hidden.append((preact * gate).astype(jnp.bfloat16))
                    column = d * hidden_size + p * panel
                    slope[:, column : column + panel] = gate * (1.0 + preact * (1.0 - gate))
                hidden = jnp.concatenate(hidden, axis=1)
                weight_copy(d, 1).wait()
                for n in range(sz.panels_out):
                    weight = weights[d, 1, n * hidden_size : (n + 1) * hidden_size, :]
                    term = (dot(hidden, weight) * sz.scale_out).astype(jnp.bfloat16)
                    total[n] = total[n] + term.astype(jnp.float32)
            output = (wide + jnp.concatenate(total, axis=1)).astype(jnp.bfloat16)
            if not backward:
                out[...] = output
                store_copies.append(pltpu.make_async_copy(slope, slope_hbm, state_sems.at[1]))
            else:
                goal = out[...].astype(jnp.float32)
                up[...] = (output.astype(jnp.float32) - goal).astype(jnp.bfloat16)
        if backward:
            second = state_sems.at[2]
            store_copies.append(pltpu.make_async_copy(up, second_hbm, second))
            store_copies[-1].start()
            up_turned = up[...].T
            total = jnp.zeros((width, sz.row_count), jnp.float32)
            for d in range(sz.shards):
                if not forward:
                    weight_copy(d, 1).wait()
                grad_hidden = jnp.zeros((hidden_size, sz.row_count), jnp.float32)
                for n in range(sz.panels_out):
                    weight = weights[d, 1, n * hidden_size : (n + 1) * hidden_size, :]
                    piece = up_turned[n * panel : (n + 1) * panel, :]
                    grad_hidden = grad_hidden + dot(weight, piece)
                local_slope = slope[:, d * hidden_size : (d + 1) * hidden_size].T
                grad_pre = (grad_hidden * sz.scale_out * local_slope).astype(jnp.bfloat16)
                if not forward:
                    weight_copy(d, 0).wait()
                term = jnp.zeros((width, sz.row_count), jnp.float32)
                for p in range(sz.panels_in):
                    weight = weights[d, 0, p * width : (p + 1) * width, :]
                    piece = grad_pre[p * panel : (p + 1) * panel, :]
                    term = term + dot(weight, piece)
                total = total + (term * sz.scale_in).astype(jnp.bfloat16).astype(jnp.float32)
            total = total.T
            exact = rows[...].astype(jnp.float32) * inverse_rms
            along = jnp.mean(total * exact, axis=1, keepdims=True)
            up_wide = up[...].astype(jnp.float32)
            out[...] = (up_wide + inverse_rms * (total - exact * along)).astype(jnp.bfloat16)
        send_copies = [
            pltpu.make_async_copy(out.at[place(leave, e)], sends[e], block_sems.at[e])
            for e in range(sz.blocks)
        ]
        for copy in send_copies:
            copy.start()
        if forward and not backward:
            store_copies[-1].start()
        for copy in send_copies + store_copies:
            copy.wait()


def chain_step(sz, step, forward, backward, holder, table, received, payloads, states):
    both = forward and backward
    kept = states[:2] if both else states
    anywhere = pl.BlockSpec(memory_space=pl.ANY)
    operands = [table, *received, *payloads, *kept]
    block = jax.ShapeDtypeStruct((sz.block_rows, sz.width), jnp.bfloat16)
    shapes = [block] * sz.blocks + [jax.ShapeDtypeStruct(s.shape, s.dtype) for s in kept]
    base = len(operands) - len(kept)
    passes = (2 if forward else 0) + (2 if backward else 0)
    results = pl.pallas_call(
        functools.partial(chain_kernel, sz, step, forward, backward, holder),
        out_shape=shapes,
        in_specs=[pl.BlockSpec(memory_space=pltpu.SMEM)] + [anywhere] * (len(operands) - 1),
        out_specs=[anywhere] * len(shapes),
        input_output_aliases={base + i: sz.blocks + i for i in range(len(kept))},
        scratch_shapes=[
            pltpu.VMEM((sz.shards, 2, sz.half, sz.panel), jnp.bfloat16),
            pltpu.VMEM((sz.row_count, sz.width), jnp.bfloat16),
            pltpu.VMEM((sz.row_count, sz.width), jnp.bfloat16),
            pltpu.VMEM((sz.row_count, sz.width), jnp.bfloat16),
            pltpu.VMEM((sz.row_count, sz.shards * sz.local_hidden), jnp.float32),
            pltpu.SemaphoreType.DMA((sz.shards, 2)),
            pltpu.SemaphoreType.DMA((sz.shards,)),
            pltpu.SemaphoreType.DMA((sz.blocks,)),
            pltpu.SemaphoreType.DMA((3,)),
        ],
        compiler_params=pltpu.CompilerParams(vmem_limit_bytes=40 * 1024 * 1024),
        cost_estimate=pl.CostEstimate(
            flops=passes * 2 * sz.row_count * sz.width * sz.local_hidden * sz.shards,
            bytes_accessed=4 * sz.half * sz.panel * sz.shards,
            transcendentals=0,
        ),
    )(*operands)
    sends, kept = list(results[: sz.blocks]), list(results[sz.blocks :])
    return sends, kept + list(states[2:]) if both else kept


def per_device(inputs, targets, weight_a, weight_b, moment_a, moment_b, routes, partners):
    replicas = lax.axis_size("replica")
    sections = lax.axis_size("section")
    shards = lax.axis_size("shard")
    replica_id = lax.axis_index("replica")
    section_id = lax.axis_index("section")
    shard_id = lax.axis_index("shard")
    row_count = inputs.shape[2]
    panel = inputs.shape[3]
    width = weight_a.shape[2]
    local_hidden = weight_a.shape[3]
    assert inputs.shape[1] == 1 and shards & (shards - 1) == 0
    assert local_hidden % panel == 0 and sections > 1
    scale_in = 1.0 / math.sqrt(width)
    scale_out = 1.0 / math.sqrt(local_hidden * shards)
    weight_in = weight_a[0, 0]
    weight_out = weight_b[0, 0]
    block_rows = row_count // replicas
    links = sections - 1
    in_kernel = block_rows % 16 == 0
    sz = Sizes(
        shards, sections, row_count, width, local_hidden, panel, replicas if in_kernel else 1
    )

    def flat(replica, section, shard):
        return (replica * sections + section) * shards + shard

    def holder(section):
        return shards // 2 - 1 + ((section ^ (section >> 1)) & 1)

    def move(array, sources, target):
        pairs = [
            (flat(r, s, j), flat(*target(r, s, j)))
            for r in range(replicas)
            for s, j in sources
        ]
        return lax.ppermute(array, axes, pairs)

    def to_holder(array, offset, active):
        return move(
            array, [(s, holder(s) ^ offset) for s in active], lambda r, s, j: (r, s, j ^ offset)
        )

    def from_holder(array, offset, active):
        return move(array, [(s, holder(s)) for s in active], lambda r, s, j: (r, s, j ^ offset))

    def between_holders(array, offset, section, step):
        return move(
            array,
            [(section, holder(section))],
            lambda r, s, j: ((r + offset) % replicas, s + step, holder(s + step)),
        )

    def across_replicas(array, offset, active):
        return move(
            array,
            [(s, j) for s in active for j in range(shards)],
            lambda r, s, j: ((r + offset) % replicas, s, j),
        )

    every = range(sections)
    others = range(1, replicas)
    is_holder = shard_id == shards // 2 - 1 + ((section_id ^ (section_id >> 1)) & 1)

    def broadcast(array, active):
        total = from_holder(array, 1, active)
        for d in range(2, shards):
            total = total + from_holder(array, d, active)
        return jnp.where(is_holder, array, total)

    edge = jnp.where(section_id == 0, inputs[0, 0], targets[0, 0])
    payload = pack(
        [weight_in, weight_out, edge],
        [width, local_hidden, row_count],
        jnp.zeros((1, 3), jnp.int32),
        panel,
    )
    payloads = [payload] + [to_holder(payload, d, every) for d in range(1, shards)]

    tables = lax.dynamic_index_in_dim(partners, section_id, 0, keepdims=False)

    def piece_of(table, offset):
        wanted = (replica_id + offset) % replicas
        return jnp.argmax(table[:, replica_id] == wanted).astype(jnp.int32)

    pieces_in = [piece_of(tables[0], e) for e in range(replicas)]
    pieces_out = [piece_of(tables[1], e) for e in range(replicas)]
    size_in = width // replicas
    size_out = local_hidden // replicas

    def piece(array, index, size, axis=0):
        return lax.dynamic_slice_in_dim(array, index * size, size, axis)

    def state_pieces(e):
        four = [weight_in, moment_a[0, 0], weight_out, moment_b[0, 0]]
        heights = [size_in, size_in, size_out, size_out]
        first_in, first_out = pieces_in[e] * size_in, pieces_out[e] * size_out
        starts = jnp.stack([first_in, first_in, first_out, first_out])[None]
        return pack(four, heights, starts, panel)

    far_states = [across_replicas(state_pieces(e), e, every) for e in others]

    def exchange_factor(array, pieces, size):
        return [across_replicas(piece(array, pieces[e], size, 1), e, every) for e in others]

    offsets = jnp.arange(replicas, dtype=jnp.int32)
    there = (replica_id + offsets) % replicas
    back = (replica_id - offsets) % replicas
    own_routes = routes[0, :, replica_id, :]
    slots = jnp.sum(
        (own_routes[:, None, :] == there[None, :, None]).astype(jnp.int32)
        * offsets[None, None, :],
        axis=2,
    )
    columns = max(replicas, sections)
    ours = (is_holder & (section_id == jnp.arange(sections))).astype(jnp.int32)

    def line(values):
        return jnp.pad(values, ((0, 0), (0, columns - values.shape[1])))

    starts = jnp.concatenate([slots, back[None]]) * block_rows
    if not in_kernel:
        starts = jnp.zeros_like(starts)
    table = jnp.concatenate([line(starts), line(ours[None])]).astype(jnp.int32)

    def send_blocks(sends, arrived, left, section, step, sign):
        if in_kernel:
            return [
                between_holders(sends[e], sign * e, section, step) for e in range(replicas)
            ]
        blocks = sends[0].reshape(replicas, block_rows, width)
        moved = jnp.zeros_like(blocks)
        for e in range(replicas):
            chosen = lax.dynamic_index_in_dim(blocks, left[e], 0, keepdims=False)
            got = between_holders(chosen, sign * e, section, step)
            moved = lax.dynamic_update_index_in_dim(moved, got, arrived[e], 0)
        return [moved.reshape(row_count, width)]

    states = [
        jnp.zeros((row_count, width), jnp.bfloat16),
        jnp.zeros((row_count, width), jnp.bfloat16),
        jnp.zeros((row_count, shards * local_hidden), jnp.float32),
    ]
    received = []
    for step in range(sections):
        last = step + 1 == sections
        sends, states = chain_step(
            sz, step, True, last, holder(step), table, received, payloads, states
        )
        if not last:
            received = send_blocks(sends, back, slots[step], step, 1, 1)

    own_rows = broadcast(states[0], every)
    inverse_rms = norm_scale(own_rows)
    normed = (own_rows.astype(jnp.float32) * inverse_rms).astype(jnp.bfloat16)
    preact = dot(normed, weight_in) * scale_in
    hidden = jax.nn.silu(preact).astype(jnp.bfloat16)
    slope = slope_of(preact)
    far_normed = exchange_factor(normed, pieces_in, size_in)
    far_hidden = exchange_factor(hidden, pieces_out, size_out)

    for step in reversed(range(1, sections)):
        if step < links:
            sends, states = chain_step(
                sz, step, False, True, holder(step), table, received, payloads, states
            )
        received = send_blocks(sends, slots[step - 1], back, step, -1, -1)
        if step == min(2, links):
            received, normed, hidden, slope, far_normed, far_hidden, far_states = (
                lax.optimization_barrier(
                    (received, normed, hidden, slope, far_normed, far_hidden, far_states)
                )
            )
    upstream = states[1]
    first_up = received[0]
    if in_kernel:
        first_up = jnp.zeros((row_count, width), jnp.bfloat16)
        for e in range(replicas):
            first_up = lax.dynamic_update_slice_in_dim(
                first_up, received[e], slots[0, e] * block_rows, 0
            )
    upstream = jnp.where(section_id == 0, first_up, upstream)
    upstream = broadcast(upstream, every)
    far_up = [across_replicas(upstream, e, every) for e in others]
    grad_hidden = dot(upstream, weight_out, contract_last) * scale_out
    grad_pre = (grad_hidden * slope).astype(jnp.bfloat16)
    far_pre = [across_replicas(grad_pre, e, every) for e in others]

    def far_part(e, which):
        sizes = [size_in, size_in, size_out, size_out]
        lengths = [size_in * local_hidden // panel] * 2 + [size_out * width // panel] * 2
        begin = sum(lengths[:which])
        return from_panels(far_states[e - 1][begin : begin + lengths[which]], sizes[which])

    def as_delta(left, right, scale):
        return (inner_rate * (dot(left, right, contract_rows) * scale)).astype(jnp.bfloat16)

    def finish(weight, moment, left, right, which, far_left, far_right, scale, pieces, size):
        new_weight, new_moment = outer_mix(
            weight.astype(jnp.float32),
            moment.astype(jnp.float32),
            as_delta(left, right, scale).astype(jnp.float32),
        )
        for e in others:
            back = replicas - e

            def mean(own_array, far_array):
                return 0.5 * (own_array.astype(jnp.float32) + far_array.astype(jnp.float32))

            index = pieces[back]
            own_left = piece(left, index, size, 1)
            part_weight, part_moment = outer_mix(
                mean(piece(weight, index, size), far_part(e, which)),
                mean(piece(moment, index, size), far_part(e, which + 1)),
                mean(
                    as_delta(own_left, right, scale),
                    as_delta(far_left[e - 1], far_right[e - 1], scale),
                ),
            )
            new_weight = lax.dynamic_update_slice_in_dim(new_weight, part_weight, index * size, 0)
            new_moment = lax.dynamic_update_slice_in_dim(new_moment, part_moment, index * size, 0)
        return new_weight[None, None], new_moment[None, None]

    new_weight_b, new_moment_b = finish(
        weight_out, moment_b[0, 0], hidden, upstream, 2, far_hidden, far_up,
        scale_out, pieces_out, size_out,
    )
    new_weight_a, new_moment_a = finish(
        weight_in, moment_a[0, 0], normed, grad_pre, 0, far_normed, far_pre,
        scale_in, pieces_in, size_in,
    )
    return (new_weight_a, new_weight_b, new_moment_a, new_moment_b)


def solution(mesh):
    placed = (
        P("replica", None, None, "shard"),
        P("replica", None, None, "shard"),
        P("replica", "section", None, "shard"),
        P("replica", "section", "shard", None),
        P("replica", "section", None, "shard"),
        P("replica", "section", "shard", None),
        P(),
        P(),
    )
    return jax.shard_map(
        per_device,
        mesh=mesh,
        in_specs=placed,
        out_specs=(
            P("replica", "section", None, "shard"),
            P("replica", "section", "shard", None),
            P("replica", "section", None, "shard"),
            P("replica", "section", "shard", None),
        ),
        check_vma=False,
    )
```

profile of v0, /device:TPU:0, one launch (start us, length us, event | category | flops | bytes accessed | tf_op | source)
XLA Modules:
  0.0 211.1 jit_solution(10138195602954511647)
XLA Ops:
  1.5 1.4 copy-done.5
  2.9 1.4 copy-done.8
  4.3 2.0 shard_map.111.refs_1_.refs_3_
  6.4 2.4 %collective-permute-start.2 = (bf16[6272,256]{1,0:T(8,128)(2,1)S(1)}, bf16[6272,256]{1,0:T(8,128)(2,1)}, u32[]{:S(2)}, u32[]{:S(2)}) collective-permute-start(bf16[6272,256]{1,0:T(8,128)(2,1)S(1)} %shard_map.111.refs_1_.refs_3_), channel_id=1, source_target_pairs={{2,1},{5,6},{9,10},{14,13},{18,17},{21,22},{25,26},{30,29}} | collective-permute-start | bytes 9633800 | tf_op jit(solution)/shard_map/ppermute | solution.py:318
  8.8 2.4 %collective-permute-start.1 = (bf16[6272,256]{1,0:T(8,128)(2,1)S(1)}, bf16[6272,256]{1,0:T(8,128)(2,1)}, u32[]{:S(2)}, u32[]{:S(2)}) collective-permute-start(bf16[6272,256]{1,0:T(8,128)(2,1)S(1)} %shard_map.111.refs_1_.refs_3_), channel_id=1, source_target_pairs={{3,1},{4,6},{8,10},{15,13},{19,17},{20,22},{24,26},{31,29}} | collective-permute-start | bytes 9633800 | tf_op jit(solution)/shard_map/ppermute | solution.py:318
  11.2 4.4 %collective-permute-start = (bf16[6272,256]{1,0:T(8,128)(2,1)S(1)}, bf16[6272,256]{1,0:T(8,128)(2,1)}, u32[]{:S(2)}, u32[]{:S(2)}) collective-permute-start(bf16[6272,256]{1,0:T(8,128)(2,1)S(1)} %shard_map.111.refs_1_.refs_3_), channel_id=1, source_target_pairs={{0,1},{7,6},{11,10},{12,13},{16,17},{23,22},{27,26},{28,29}} | collective-permute-start | bytes 9633800 | tf_op jit(solution)/shard_map/ppermute | solution.py:318
  18.5 1.4 copy-done.6
  19.9 1.4 copy-done.9
  21.3 1.4 copy-done.12
  22.8 1.4 copy-done.14
  24.2 2.8 %shard_map.117 = bf16[6144,256]{1,0:T(8,128)(2,1)} custom-call(s32[1,4]{1,0:T(1,128)S(1)} %add_bitcast_fusion.starts, bf16[1024,768]{1,0:T(8,128)(2,1)S(1)} %bitcast.83, bf16[1024,768]{1,0:T(8,128)(2,1)S(1)} %bitcast.84, bf16[768,1024]{1,0:T(8,128)(2,1)S(1)} %bitcast.81, bf16[768,1024]{1,0:T(8,128)(2,1)S(1)} %bitcast.85), custom_call_target="tpu_custom_call" | custom-call | bytes 6291456 | tf_op jit(solution)/shard_map/pallas_call | solution.py:77
  26.9 1.6 collective-permute-start.18
  28.8 53.7 %collective-permute-done.refs_2_.refs_4_ = bf16[6272,256]{1,0:T(8,128)(2,1)} collective-permute-done((bf16[6272,256]{1,0:T(8,128)(2,1)S(1)}, bf16[6272,256]{1,0:T(8,128)(2,1)}, u32[]{:S(2)}, u32[]{:S(2)}) %collective-permute-start) | collective-permute-done | bytes 3211296 | tf_op jit(solution)/shard_map/ppermute | solution.py:318
  97.6 15.7 %collective-permute-done.13 = bf16[128,1024]{1,0:T(8,128)(2,1)} collective-permute-done((bf16[128,1024]{1,0:T(8,128)(2,1)}, bf16[128,1024]{1,0:T(8,128)(2,1)}, u32[]{:S(2)}, u32[]{:S(2)}) %collective-permute-start.13) | collective-permute-done | bytes 262176 | tf_op jit(solution)/shard_map/ppermute | solution.py:318
  115.6 1.5 collective-permute-start.16
  125.6 3.1 %collective-permute-done.17 = bf16[128,384]{1,0:T(8,128)(2,1)} collective-permute-done((bf16[128,384]{1,0:T(8,128)(2,1)}, bf16[128,384]{1,0:T(8,128)(2,1)}, u32[]{:S(2)}, u32[]{:S(2)}) %collective-permute-start.17) | collective-permute-done | bytes 98336 | tf_op jit(solution)/shard_map/ppermute | solution.py:318
  128.7 1.4 copy-done.4
  132.4 1.5 fusion.43
  136.8 1.7 fusion.42
  138.5 57.1 %collective-permute-done.21 = bf16[128,1024]{1,0:T(8,128)(2,1)S(1)} collective-permute-done((bf16[128,1024]{1,0:T(8,128)(2,1)S(1)}, bf16[128,1024]{1,0:T(8,128)(2,1)S(1)}, u32[]{:S(2)}, u32[]{:S(2)}) %collective-permute-start.21) | collective-permute-done | bytes 262176 | tf_op jit(solution)/shard_map/ppermute | solution.py:318
  198.8 1.5 collective-permute-start.24
  201.8 3.4 %collective-permute-done.24 = bf16[128,768]{1,0:T(8,128)(2,1)S(1)} collective-permute-done((bf16[128,768]{1,0:T(8,128)(2,1)S(1)}, bf16[128,768]{1,0:T(8,128)(2,1)S(1)}, u32[]{:S(2)}, u32[]{:S(2)}) %collective-permute-start.24) | collective-permute-done | bytes 196640 | tf_op jit(solution)/shard_map/ppermute | solution.py:318
  205.3 2.0 fusion.29
  207.3 2.1 fusion.27
  (130 shorter events, 38.6 us)
Async XLA Ops:
  6.4 22.3 %collective-permute-start.2 = (bf16[6272,256]{1,0:T(8,128)(2,1)S(1)}, bf16[6272,256]{1,0:T(8,128)(2,1)}, u32[]{:S(2)}, u32[]{:S(2)}) collective-permute-start(bf16[6272,256]{1,0:T(8,128)(2,1)S(1)} %shard_map.111.refs_1_.refs_3_), channel_id=1, source_target_pairs={{2,1},{5,6},{9,10},{14,13},{18,17},{21,22},{25,26},{30,29}} | collective-permute-start | bytes 9633800 | tf_op jit(solution)/shard_map/ppermute | solution.py:318
  8.8 20.0 %collective-permute-start.1 = (bf16[6272,256]{1,0:T(8,128)(2,1)S(1)}, bf16[6272,256]{1,0:T(8,128)(2,1)}, u32[]{:S(2)}, u32[]{:S(2)}) collective-permute-start(bf16[6272,256]{1,0:T(8,128)(2,1)S(1)} %shard_map.111.refs_1_.refs_3_), channel_id=1, source_target_pairs={{3,1},{4,6},{8,10},{15,13},{19,17},{20,22},{24,26},{31,29}} | collective-permute-start | bytes 9633800 | tf_op jit(solution)/shard_map/ppermute | solution.py:318
  11.2 71.3 %collective-permute-start = (bf16[6272,256]{1,0:T(8,128)(2,1)S(1)}, bf16[6272,256]{1,0:T(8,128)(2,1)}, u32[]{:S(2)}, u32[]{:S(2)}) collective-permute-start(bf16[6272,256]{1,0:T(8,128)(2,1)S(1)} %shard_map.111.refs_1_.refs_3_), channel_id=1, source_target_pairs={{0,1},{7,6},{11,10},{12,13},{16,17},{23,22},{27,26},{28,29}} | collective-permute-start | bytes 9633800 | tf_op jit(solution)/shard_map/ppermute | solution.py:318
  26.9 98.7 %collective-permute-start.18 = (bf16[6144,256]{1,0:T(8,128)(2,1)}, bf16[6144,256]{1,0:T(8,128)(2,1)}, u32[]{:S(2)}, u32[]{:S(2)}) collective-permute-start(bf16[6144,256]{1,0:T(8,128)(2,1)} %shard_map.117), channel_id=1, source_target_pairs={{0,16},{1,17},{2,18},{3,19},{4,20},{5,21},{6,22},{7,23},{8,24},{9,... | collective-permute-start | bytes 9437192 | tf_op jit(solution)/shard_map/ppermute | solution.py:318
  84.1 1.4 collective-permute-start.3
  84.8 0.7 collective-permute-start.4
  86.3 1.4 collective-permute-start.5
  88.4 1.4 collective-permute-start.7
  92.1 4.9 %collective-permute-start.15 = (bf16[128,1024]{1,0:T(8,128)(2,1)}, bf16[128,1024]{1,0:T(8,128)(2,1)}, u32[]{:S(2)}, u32[]{:S(2)}) collective-permute-start(bf16[128,1024]{1,0:T(8,128)(2,1)} %get-tuple-element.57.refs_7_), channel_id=1, source_target_pairs={{1,2},{6,5},{10,9},{13,14},{17,18},{22,21},{26,25},{29,30}} | collective-permute-start | bytes 786440 | tf_op jit(solution)/shard_map/ppermute | solution.py:318
  93.5 4.2 %collective-permute-start.14 = (bf16[128,1024]{1,0:T(8,128)(2,1)}, bf16[128,1024]{1,0:T(8,128)(2,1)}, u32[]{:S(2)}, u32[]{:S(2)}) collective-permute-start(bf16[128,1024]{1,0:T(8,128)(2,1)} %get-tuple-element.57.refs_7_), channel_id=1, source_target_pairs={{1,3},{6,4},{10,8},{13,15},{17,19},{22,20},{26,24},{29,31}} | collective-permute-start | bytes 786440 | tf_op jit(solution)/shard_map/ppermute | solution.py:318
  94.8 18.5 %collective-permute-start.13 = (bf16[128,1024]{1,0:T(8,128)(2,1)}, bf16[128,1024]{1,0:T(8,128)(2,1)}, u32[]{:S(2)}, u32[]{:S(2)}) collective-permute-start(bf16[128,1024]{1,0:T(8,128)(2,1)} %get-tuple-element.57.refs_7_), channel_id=1, source_target_pairs={{1,0},{6,7},{10,11},{13,12},{17,16},{22,23},{26,27},{29,28}} | collective-permute-start | bytes 786440 | tf_op jit(solution)/shard_map/ppermute | solution.py:318
  96.1 20.9 %collective-permute-start.9 = (bf16[64,1024]{1,0:T(8,128)(2,1)}, bf16[64,1024]{1,0:T(8,128)(2,1)S(1)}, u32[]{:S(2)}, u32[]{:S(2)}) collective-permute-start(bf16[64,1024]{1,0:T(8,128)(2,1)} %copy-done.17), channel_id=1, source_target_pairs={{13,10},{29,26}} | collective-permute-start | bytes 393224 | tf_op jit(solution)/shard_map/ppermute | solution.py:318
  97.0 20.1 %collective-permute-start.10 = (bf16[64,1024]{1,0:T(8,128)(2,1)}, bf16[64,1024]{1,0:T(8,128)(2,1)S(1)}, u32[]{:S(2)}, u32[]{:S(2)}) collective-permute-start(bf16[64,1024]{1,0:T(8,128)(2,1)} %copy-done.16), channel_id=1, source_target_pairs={{13,26},{29,10}} | collective-permute-start | bytes 393224 | tf_op jit(solution)/shard_map/ppermute | solution.py:318
  115.6 13.1 %collective-permute-start.16 = (bf16[128,512]{1,0:T(8,128)(2,1)}, bf16[128,512]{1,0:T(8,128)(2,1)}, u32[]{:S(2)}, u32[]{:S(2)}) collective-permute-start(bf16[128,512]{1,0:T(8,128)(2,1)} %constant_dynamic-slice_fusion.2), channel_id=1, source_target_pairs={{0,16},{1,17},{2,18},{3,19},{4,20},{5,21},{6,22},{7,23},{8,24},{9,... | collective-permute-start | bytes 393224 | tf_op jit(solution)/shard_map/ppermute | solution.py:318
  117.9 10.8 %collective-permute-start.11 = (bf16[64,1024]{1,0:T(8,128)(2,1)}, bf16[64,1024]{1,0:T(8,128)(2,1)}, u32[]{:S(2)}, u32[]{:S(2)}) collective-permute-start(bf16[64,1024]{1,0:T(8,128)(2,1)} %get-tuple-element.60), channel_id=1, source_target_pairs={{10,6},{26,22}} | collective-permute-start | bytes 393224 | tf_op jit(solution)/shard_map/ppermute | solution.py:318
  119.2 9.5 %collective-permute-start.12 = (bf16[64,1024]{1,0:T(8,128)(2,1)}, bf16[64,1024]{1,0:T(8,128)(2,1)}, u32[]{:S(2)}, u32[]{:S(2)}) collective-permute-start(bf16[64,1024]{1,0:T(8,128)(2,1)} %get-tuple-element.61), channel_id=1, source_target_pairs={{10,22},{26,6}} | collective-permute-start | bytes 393224 | tf_op jit(solution)/shard_map/ppermute | solution.py:318
  123.1 5.5 %collective-permute-start.17 = (bf16[128,384]{1,0:T(8,128)(2,1)}, bf16[128,384]{1,0:T(8,128)(2,1)}, u32[]{:S(2)}, u32[]{:S(2)}) collective-permute-start(bf16[128,384]{1,0:T(8,128)(2,1)} %constant_dynamic-slice_fusion), channel_id=1, source_target_pairs={{0,16},{1,17},{2,18},{3,19},{4,20},{5,21},{6,22},{7,23},{8,24},{9,... | collective-permute-start | bytes 294920 | tf_op jit(solution)/shard_map/ppermute | solution.py:318
  131.0 2.8 %collective-permute-start.19 = (bf16[64,1024]{1,0:T(8,128)(2,1)S(1)}, bf16[64,1024]{1,0:T(8,128)(2,1)S(1)}, u32[]{:S(2)}, u32[]{:S(2)}) collective-permute-start(bf16[64,1024]{1,0:T(8,128)(2,1)S(1)} %get-tuple-element.70), channel_id=1, source_target_pairs={{6,1},{22,17}} | collective-permute-start | bytes 393224 | tf_op jit(solution)/shard_map/ppermute | solution.py:318
  131.7 2.2 %collective-permute-start.20 = (bf16[64,1024]{1,0:T(8,128)(2,1)S(1)}, bf16[64,1024]{1,0:T(8,128)(2,1)S(1)}, u32[]{:S(2)}, u32[]{:S(2)}) collective-permute-start(bf16[64,1024]{1,0:T(8,128)(2,1)S(1)} %get-tuple-element.71), channel_id=1, source_target_pairs={{6,17},{22,1}} | collective-permute-start | bytes 393224 | tf_op jit(solution)/shard_map/ppermute | solution.py:318
  134.0 4.5 %collective-permute-start.23 = (bf16[128,1024]{1,0:T(8,128)(2,1)S(1)}, bf16[128,1024]{1,0:T(8,128)(2,1)S(1)}, u32[]{:S(2)}, u32[]{:S(2)}) collective-permute-start(bf16[128,1024]{1,0:T(8,128)(2,1)S(1)} %broadcast_select_fusion), channel_id=1, source_target_pairs={{1,2},{6,5},{10,9},{13,14},{17,18},{22,21},{26,25},{29,30}} | collective-permute-start | bytes 786440 | tf_op jit(solution)/shard_map/ppermute | solution.py:318
  134.8 3.7 %collective-permute-start.22 = (bf16[128,1024]{1,0:T(8,128)(2,1)S(1)}, bf16[128,1024]{1,0:T(8,128)(2,1)S(1)}, u32[]{:S(2)}, u32[]{:S(2)}) collective-permute-start(bf16[128,1024]{1,0:T(8,128)(2,1)S(1)} %broadcast_select_fusion), channel_id=1, source_target_pairs={{1,3},{6,4},{10,8},{13,15},{17,19},{22,20},{26,24},{29,31}} | collective-permute-start | bytes 786440 | tf_op jit(solution)/shard_map/ppermute | solution.py:318
  135.5 60.1 %collective-permute-start.21 = (bf16[128,1024]{1,0:T(8,128)(2,1)S(1)}, bf16[128,1024]{1,0:T(8,128)(2,1)S(1)}, u32[]{:S(2)}, u32[]{:S(2)}) collective-permute-start(bf16[128,1024]{1,0:T(8,128)(2,1)S(1)} %broadcast_select_fusion), channel_id=1, source_target_pairs={{1,0},{6,7},{10,11},{13,12},{17,16},{22,23},{26,27},{29,28}} | collective-permute-start | bytes 786440 | tf_op jit(solution)/shard_map/ppermute | solution.py:318
  195.7 11.6 %collective-permute-start.25 = (bf16[128,1024]{1,0:T(8,128)(2,1)S(1)}, bf16[128,1024]{1,0:T(8,128)(2,1)S(1)}, u32[]{:S(2)}, u32[]{:S(2)}) collective-permute-start(bf16[128,1024]{1,0:T(8,128)(2,1)S(1)} %add_select_fusion), channel_id=1, source_target_pairs={{0,16},{1,17},{2,18},{3,19},{4,20},{5,21},{6,22},{7,23},{8,24},{9,... | collective-permute-start | bytes 786440 | tf_op jit(solution)/shard_map/ppermute | solution.py:318
  198.8 6.5 %collective-permute-start.24 = (bf16[128,768]{1,0:T(8,128)(2,1)S(1)}, bf16[128,768]{1,0:T(8,128)(2,1)S(1)}, u32[]{:S(2)}, u32[]{:S(2)}) collective-permute-start(bf16[128,768]{1,0:T(8,128)(2,1)S(1)} %fusion.25), channel_id=1, source_target_pairs={{0,16},{1,17},{2,18},{3,19},{4,20},{5,21},{6,22},{7,23},{8,24},{9,... | collective-permute-start | bytes 589832 | tf_op jit(solution)/shard_map/ppermute | solution.py:318
  (30 other events, 285.4 us)
where the time goes:
time: 212 us; the launch traced here: 211 us
  waiting for transfers between devices  133 us (63%)
  starting transfers between devices  31.2 us (15%)
  local copies, waits for them, and re-layouts  19.7 us (9%)
  Pallas kernels  9.78 us (5%)
  matrix products  9.2 us (4%)
  other arithmetic  4.17 us (2%)
  between operations  3.99 us (2%)
    ppermute x26, waiting for transfers between devices, move(): return lax.ppermute(array, axes, pairs)  133 us
    ppermute x26, starting transfers between devices, move(): return lax.ppermute(array, axes, pairs)  31.2 us
    unnamed x56, local copies, waits for them, and re-layouts  13.6 us
    dot_general x8, matrix products, dot(): lax.dot_general(left, right, dims, preferred_element_type=jnp.float32)  9.2 us
    pallas_call x6, Pallas kernels, chain_step(): pl.pallas_call(functools.partial(chain_kernel, sz, step, forward, backwar...  4.99 us
    pallas_call x2, Pallas kernels, pack(): pl.pallas_call(functools.partial(pack_kernel, heights, panel), out_shape=...  4.8 us
  transfers between devices with their start and end apart: 26, of which 5 were waited for; matrix products, arithmetic and copies ran while one was open for 8% of the time, Pallas kernels for 3%

commit v1 on v0

v1 whole, which is shorter than its diff:
```python
import functools
import math

import jax
import jax.numpy as jnp
from jax import lax
from jax.experimental import pallas as pl
from jax.experimental.pallas import tpu as pltpu
from jax.sharding import PartitionSpec as P

epsilon = 1e-05
inner_rate = 0.5
momentum_decay = 0.9
outer_rate = 0.7

axes = ("replica", "section", "shard")
contract_rows = (((0,), (0,)), ((), ()))
contract_last = (((1,), (1,)), ((), ()))


def norm_scale(rows):
    wide = rows.astype(jnp.float32)
    return lax.rsqrt(jnp.mean(wide * wide, axis=1, keepdims=True) + epsilon)


def dot(left, right, dims=(((1,), (0,)), ((), ()))):
    return lax.dot_general(left, right, dims, preferred_element_type=jnp.float32)


def outer_mix(weight, moment, delta):
    new_moment = momentum_decay * moment + delta
    new_weight = weight - outer_rate * (momentum_decay * new_moment + delta)
    return new_weight.astype(jnp.bfloat16), new_moment.astype(jnp.bfloat16)


def slope_of(preact):
    gate = jax.nn.sigmoid(preact)
    return gate * (1.0 + preact * (1.0 - gate))


def from_panels(array, rows):
    count = array.shape[0] // rows
    return jnp.concatenate([array[i * rows : (i + 1) * rows] for i in range(count)], axis=1)


def pack_kernel(heights, panel, starts, *refs):
    sources, (packed, buffer, read_sems, write_sems) = refs[:-4], refs[-4:]
    reads, writes = [], []
    place = 0
    for i, (source, height) in enumerate(zip(sources, heights)):
        rows = pl.ds(pl.multiple_of(starts[0, i], height), height)
        for column in range(0, source.shape[1], panel):
            k = len(reads)
            there = pl.ds(place, height)
            reads.append(
                pltpu.make_async_copy(
                    source.at[rows, pl.ds(column, panel)], buffer.at[there], read_sems.at[k]
                )
            )
            writes.append(
                pltpu.make_async_copy(buffer.at[there], packed.at[there], write_sems.at[k])
            )
            place += height
    for copy in reads:
        copy.start()
    for read, write in zip(reads, writes):
        read.wait()
        write.start()
    for copy in writes:
        copy.wait()


def pack(arrays, heights, starts, panel):
    counts = [array.shape[1] // panel for array in arrays]
    total = sum(count * height for count, height in zip(counts, heights))
    anywhere = pl.BlockSpec(memory_space=pl.ANY)
    return pl.pallas_call(
        functools.partial(pack_kernel, heights, panel),
        out_shape=jax.ShapeDtypeStruct((total, panel), arrays[0].dtype),
        in_specs=[pl.BlockSpec(memory_space=pltpu.SMEM)] + [anywhere] * len(arrays),
        out_specs=anywhere,
        scratch_shapes=[
            pltpu.VMEM((total, panel), arrays[0].dtype),
            pltpu.SemaphoreType.DMA((sum(counts),)),
            pltpu.SemaphoreType.DMA((sum(counts),)),
        ],
        compiler_params=pltpu.CompilerParams(vmem_limit_bytes=16 * 1024 * 1024),
        cost_estimate=pl.CostEstimate(
            flops=0, bytes_accessed=4 * total * panel, transcendentals=0
        ),
    )(starts, *arrays)


class Sizes:
    def __init__(self, sections, row_count, width, local_hidden, panel, hidden_total, blocks):
        self.sections, self.row_count = sections, row_count
        self.width, self.local_hidden, self.panel = width, local_hidden, panel
        self.blocks = blocks
        self.block_rows = row_count // blocks
        self.panels_in = local_hidden // panel
        self.panels_out = width // panel
        self.half = width * self.panels_in
        self.scale_in = 1.0 / math.sqrt(width)
        self.scale_out = 1.0 / math.sqrt(hidden_total)


def chain_kernel(sz, step, forward, counts, *refs):
    refs = list(refs)

    def take(count):
        taken = refs[:count]
        del refs[:count]
        return taken

    (table,) = take(1)
    received, edges, payloads = take(counts[0]), take(counts[1]), take(2)
    take(3)
    sends = take(counts[2])
    rows_hbm, up_hbm, slope_hbm = take(3)
    weights, landing, rows, up, out, slope = take(6)
    weight_sems, block_sems, edge_sems, send_sems, state_sems = take(5)
    panel, width, hidden_size = sz.panel, sz.width, sz.local_hidden
    links = sz.sections - 1
    whole = pl.ds(0, sz.row_count)

    def weight_copy(d, which):
        return pltpu.make_async_copy(
            payloads[d].at[pl.ds(which * sz.half, sz.half)],
            weights.at[d, which],
            weight_sems.at[d, which],
        )

    def place(line, e):
        return pl.ds(pl.multiple_of(table[line, e], sz.block_rows), sz.block_rows)

    @pl.when(table[links + 1, step] == 1)
    def _():
        sequence = [(d, which if forward else 1 - which) for d in range(2) for which in range(2)]
        arrive = links if forward else step
        first_copies = []
        for i, source in enumerate(received):
            e, a = divmod(i, 2)
            rows_there = whole if len(received) == 2 else place(arrive, e)
            first_copies.append(
                pltpu.make_async_copy(source, landing.at[a, rows_there], block_sems.at[i])
            )
        if edges:
            edge_refs = [payload.at[pl.ds(2 * sz.half, sz.row_count)] for payload in payloads]
            for d, source in enumerate(edge_refs + edges):
                column = pl.ds(pl.multiple_of(table[links + 2, d], panel), panel)
                first_copies.append(
                    pltpu.make_async_copy(source, out.at[:, column], edge_sems.at[d])
                )
        if not forward:
            first_copies.append(pltpu.make_async_copy(rows_hbm, rows, state_sems.at[0]))
            first_copies.append(pltpu.make_async_copy(slope_hbm, slope, state_sems.at[1]))
        for copy in first_copies:
            copy.start()
        for item in sequence[:2]:
            weight_copy(*item).start()

        def arrived(item):
            weight_copy(*item).wait()
            later = sequence.index(item) + 2
            if later < len(sequence):
                weight_copy(*sequence[later]).start()

        for copy in first_copies:
            copy.wait()
        if received:
            total = landing[0].astype(jnp.float32) + landing[1].astype(jnp.float32)
            total = total.astype(jnp.bfloat16)
        if forward:
            rows[...] = total if received else out[...]
        elif edges:
            goal = out[...].astype(jnp.float32)
            up[...] = (total.astype(jnp.float32) - goal).astype(jnp.bfloat16)
        else:
            up[...] = total
        fresh, fresh_hbm = (rows, rows_hbm) if forward else (up, up_hbm)
        store_copies = [pltpu.make_async_copy(fresh, fresh_hbm, state_sems.at[2])]
        store_copies[0].start()

        wide = rows[...].astype(jnp.float32)
        inverse_rms = lax.rsqrt(jnp.mean(wide * wide, axis=1, keepdims=True) + epsilon)
        leads = table[links + 2, 2] > table[links + 2, 0]
        if forward:
            normed = (wide * inverse_rms).astype(jnp.bfloat16)
            total = [jnp.zeros((sz.row_count, panel), jnp.float32) for _ in range(sz.panels_out)]
            for d in range(2):
                arrived((d, 0))
                hidden = []
                for p in range(sz.panels_in):
                    weight = weights[d, 0, p * width : (p + 1) * width, :]
                    preact = dot(normed, weight) * sz.scale_in
                    gate = jax.nn.sigmoid(preact)
                    hidden.append((preact * gate).astype(jnp.bfloat16))
                    column = d * hidden_size + p * panel
                    slope[:, column : column + panel] = gate * (1.0 + preact * (1.0 - gate))
                hidden = jnp.concatenate(hidden, axis=1)
                arrived((d, 1))
                for n in range(sz.panels_out):
                    weight = weights[d, 1, n * hidden_size : (n + 1) * hidden_size, :]
                    total[n] = total[n] + dot(hidden, weight)
            total = jnp.concatenate(total, axis=1) * sz.scale_out
            out[...] = (total + jnp.where(leads, wide, 0.0)).astype(jnp.bfloat16)
            store_copies.append(pltpu.make_async_copy(slope, slope_hbm, state_sems.at[1]))
        else:
            up_turned = up[...].T
            total = jnp.zeros((width, sz.row_count), jnp.float32)
            for d in range(2):
                arrived((d, 1))
                grad_hidden = jnp.zeros((hidden_size, sz.row_count), jnp.float32)
                for n in range(sz.panels_out):
                    weight = weights[d, 1, n * hidden_size : (n + 1) * hidden_size, :]
                    piece = up_turned[n * panel : (n + 1) * panel, :]
                    grad_hidden = grad_hidden + dot(weight, piece)
                local_slope = slope[:, d * hidden_size : (d + 1) * hidden_size].T
                grad_pre = (grad_hidden * sz.scale_out * local_slope).astype(jnp.bfloat16)
                arrived((d, 0))
                for p in range(sz.panels_in):
                    weight = weights[d, 0, p * width : (p + 1) * width, :]
                    piece = grad_pre[p * panel : (p + 1) * panel, :]
                    total = total + dot(weight, piece)
            total = total.T * sz.scale_in
            exact = wide * inverse_rms
            along = jnp.mean(total * exact, axis=1, keepdims=True)
            own = jnp.where(leads, up[...].astype(jnp.float32), 0.0)
            out[...] = (own + inverse_rms * (total - exact * along)).astype(jnp.bfloat16)
        leave = step if forward else links
        send_copies = []
        for e, target in enumerate(sends):
            rows_here = whole if len(sends) == 1 else place(leave, e)
            send_copies.append(
                pltpu.make_async_copy(out.at[rows_here], target, send_sems.at[e])
            )
        for copy in send_copies + store_copies[1:]:
            copy.start()
        for copy in send_copies + store_copies:
            copy.wait()


def chain_step(sz, step, forward, table, received, edges, payloads, states):
    last = step + 1 == sz.sections
    count = 1 if forward and last else sz.blocks
    anywhere = pl.BlockSpec(memory_space=pl.ANY)
    operands = [table, *received, *edges, *payloads, *states]
    block = jax.ShapeDtypeStruct((sz.row_count // count, sz.width), jnp.bfloat16)
    shapes = [block] * count + [jax.ShapeDtypeStruct(s.shape, s.dtype) for s in states]
    base = len(operands) - len(states)
    whole = (sz.row_count, sz.width)
    results = pl.pallas_call(
        functools.partial(
            chain_kernel, sz, step, forward, (len(received), len(edges), count)
        ),
        out_shape=shapes,
        in_specs=[pl.BlockSpec(memory_space=pltpu.SMEM)] + [anywhere] * (len(operands) - 1),
        out_specs=[anywhere] * len(shapes),
        input_output_aliases={base + i: count + i for i in range(len(states))},
        scratch_shapes=[
            pltpu.VMEM((2, 2, sz.half, sz.panel), jnp.bfloat16),
            pltpu.VMEM((2,) + whole, jnp.bfloat16),
            pltpu.VMEM(whole, jnp.bfloat16),
            pltpu.VMEM(whole, jnp.bfloat16),
            pltpu.VMEM(whole, jnp.bfloat16),
            pltpu.VMEM((sz.row_count, 2 * sz.local_hidden), jnp.float32),
            pltpu.SemaphoreType.DMA((2, 2)),
            pltpu.SemaphoreType.DMA((max(1, len(received)),)),
            pltpu.SemaphoreType.DMA((4,)),
            pltpu.SemaphoreType.DMA((count,)),
            pltpu.SemaphoreType.DMA((3,)),
        ],
        compiler_params=pltpu.CompilerParams(vmem_limit_bytes=32 * 1024 * 1024),
        cost_estimate=pl.CostEstimate(
            flops=8 * sz.row_count * sz.width * sz.local_hidden,
            bytes_accessed=8 * sz.half * sz.panel,
            transcendentals=0,
        ),
    )(*operands)
    return list(results[:count]), list(results[count:])


def per_device(inputs, targets, weight_a, weight_b, moment_a, moment_b, routes, partners):
    replicas = lax.axis_size("replica")
    sections = lax.axis_size("section")
    shards = lax.axis_size("shard")
    replica_id = lax.axis_index("replica")
    section_id = lax.axis_index("section")
    shard_id = lax.axis_index("shard")
    row_count = inputs.shape[2]
    panel = inputs.shape[3]
    width = weight_a.shape[2]
    local_hidden = weight_a.shape[3]
    assert inputs.shape[1] == 1 and shards == 4
    assert local_hidden % panel == 0 and sections > 2
    hidden_total = local_hidden * shards
    scale_in = 1.0 / math.sqrt(width)
    scale_out = 1.0 / math.sqrt(hidden_total)
    weight_in = weight_a[0, 0]
    weight_out = weight_b[0, 0]
    block_rows = row_count // replicas
    links = sections - 1
    in_kernel = block_rows % 16 == 0
    blocks = replicas if in_kernel else 1
    sz = Sizes(sections, row_count, width, local_hidden, panel, hidden_total, blocks)

    def flat(replica, section, shard):
        return (replica * sections + section) * shards + shard

    def turn(section):
        return (section ^ (section >> 1)) & 1

    def holders(section):
        return [j for j in range(shards) if (j & 1) != turn(section)]

    def move(array, sources, target):
        pairs = [
            (flat(r, s, j), flat(*target(r, s, j)))
            for r in range(replicas)
            for s, j in sources
        ]
        return lax.ppermute(array, axes, pairs)

    def holder_sources(active):
        return [(s, j) for s in active for j in holders(s)]

    def to_holders(array, offset, active):
        sources = [(s, j ^ offset) for s, j in holder_sources(active)]
        return move(array, sources, lambda r, s, j: (r, s, j ^ offset))

    def from_holders(array, offset, active):
        return move(array, holder_sources(active), lambda r, s, j: (r, s, j ^ offset))

    def between_holders(array, offset, other_half, section, step):
        shift = turn(section) ^ turn(section + step) ^ (2 * other_half)
        return move(
            array,
            holder_sources([section]),
            lambda r, s, j: ((r + offset) % replicas, s + step, j ^ shift),
        )

    def across_replicas(array, offset, active):
        return move(
            array,
            [(s, j) for s in active for j in range(shards)],
            lambda r, s, j: ((r + offset) % replicas, s, j),
        )

    every = range(sections)
    others = range(1, replicas)
    is_holder = (shard_id & 1) != turn(section_id)

    edge = jnp.where(section_id == 0, inputs[0, 0], targets[0, 0])
    edges = [to_holders(edge, d, [0, links]) for d in (2, 3)]
    payload = pack(
        [weight_in, weight_out, edge],
        [width, local_hidden, row_count],
        jnp.zeros((1, 3), jnp.int32),
        panel,
    )
    payloads = [payload, to_holders(payload, 1, every)]

    tables = lax.dynamic_index_in_dim(partners, section_id, 0, keepdims=False)

    def piece_of(table, offset):
        wanted = (replica_id + offset) % replicas
        return jnp.argmax(table[:, replica_id] == wanted).astype(jnp.int32)

    pieces_in = [piece_of(tables[0], e) for e in range(replicas)]
    pieces_out = [piece_of(tables[1], e) for e in range(replicas)]
    size_in = width // replicas
    size_out = local_hidden // replicas

    def piece(array, index, size, axis=0):
        return lax.dynamic_slice_in_dim(array, index * size, size, axis)

    def state_pieces(weight, moment, index, size):
        starts = jnp.broadcast_to(index * size, (1, 2))
        return pack([weight, moment], [size, size], starts, panel)

    def exchange(arrays, active):
        return [across_replicas(array, e, active) for e, array in zip(others, arrays)]

    packed_in = [state_pieces(weight_in, moment_a[0, 0], pieces_in[e], size_in) for e in others]
    packed_out = [
        state_pieces(weight_out, moment_b[0, 0], pieces_out[e], size_out) for e in others
    ]
    early = range(sections // 2, sections)
    late = range(sections // 2)
    far_states_in = exchange(packed_in, every)
    far_states_out = exchange(packed_out, early)

    offsets = jnp.arange(replicas, dtype=jnp.int32)
    there = (replica_id + offsets) % replicas
    back = (replica_id - offsets) % replicas
    own_routes = routes[0, :, replica_id, :]
    slots = jnp.sum(
        (own_routes[:, None, :] == there[None, :, None]).astype(jnp.int32)
        * offsets[None, None, :],
        axis=2,
    )
    columns = max(replicas, sections, shards)
    ours = (is_holder & (section_id == jnp.arange(sections))).astype(jnp.int32)
    features = (shard_id ^ jnp.arange(shards, dtype=jnp.int32)) * panel

    def line(values):
        return jnp.pad(values, ((0, 0), (0, columns - values.shape[1])))

    starts = jnp.concatenate([slots, back[None]]) * block_rows
    if not in_kernel:
        starts = jnp.zeros_like(starts)
    table = jnp.concatenate([line(starts), line(ours[None]), line(features[None])])
    table = table.astype(jnp.int32)

    def send_blocks(sends, arrived, left, section, step):
        sign = step
        if in_kernel:
            return [
                between_holders(sends[e], sign * e, a, section, step)
                for e in range(replicas)
                for a in range(2)
            ]
        parts = sends[0].reshape(replicas, block_rows, width)
        moved = [jnp.zeros_like(parts), jnp.zeros_like(parts)]
        for e in range(replicas):
            chosen = lax.dynamic_index_in_dim(parts, left[e], 0, keepdims=False)
            for a in range(2):
                got = between_holders(chosen, sign * e, a, section, step)
                moved[a] = lax.dynamic_update_index_in_dim(moved[a], got, arrived[e], 0)
        return [one.reshape(row_count, width) for one in moved]

    states = [
        jnp.zeros((row_count, width), jnp.bfloat16),
        jnp.zeros((row_count, width), jnp.bfloat16),
        jnp.zeros((row_count, 2 * local_hidden), jnp.float32),
    ]
    received = []
    for step in every:
        sends, states = chain_step(
            sz, step, True, table, received, edges if step == 0 else [], payloads, states
        )
        if step < links:
            received = send_blocks(sends, back, slots[step], step, 1)
        else:
            received = [sends[0], from_holders(sends[0], 2, [links])]
        if step == len(late) - 1:
            received, packed_out = lax.optimization_barrier((received, packed_out))
            far_late = exchange(packed_out, late)

    for step in reversed(range(1, sections)):
        sends, states = chain_step(
            sz, step, False, table, received, edges if step == links else [], payloads, states
        )
        received = send_blocks(sends, slots[step - 1], back, step, -1)

    known, sends = lax.optimization_barrier((jnp.concatenate(states[:2]), sends))
    known = jnp.where(is_holder, known, from_holders(known, 1, every))
    own_rows, upstream = known[:row_count], known[row_count:]
    inverse_rms = norm_scale(own_rows)
    normed = (own_rows.astype(jnp.float32) * inverse_rms).astype(jnp.bfloat16)
    preact = dot(normed, weight_in) * scale_in
    hidden = jax.nn.silu(preact).astype(jnp.bfloat16)
    slope = slope_of(preact)

    def before_slope(upstream):
        grad_hidden = dot(upstream, weight_out, contract_last) * scale_out
        return (grad_hidden * slope).astype(jnp.bfloat16)

    grad_pre = before_slope(upstream)
    far_normed = exchange([piece(normed, pieces_in[e], size_in, 1) for e in others], every)
    far_hidden = exchange([piece(hidden, pieces_out[e], size_out, 1) for e in others], every)
    rest = range(1, sections)
    far_up = exchange([upstream] * len(others), rest)
    far_pre = exchange([grad_pre] * len(others), rest)

    halves = []
    for a in range(2):
        half = received[a]
        if in_kernel:
            half = jnp.zeros((row_count, width), jnp.bfloat16)
            for e in range(replicas):
                half = lax.dynamic_update_slice_in_dim(
                    half, received[2 * e + a], slots[0, e] * block_rows, 0
                )
        halves.append(half.astype(jnp.float32))
    first_up = (halves[0] + halves[1]).astype(jnp.bfloat16)
    first_up = jnp.where(is_holder, first_up, from_holders(first_up, 1, [0]))
    first_pre = before_slope(first_up)
    here = section_id == 0

    def merge(first, other):
        return jnp.where(here, first, other)

    far_up = [
        merge(one, two) for one, two in zip(exchange([first_up] * len(others), [0]), far_up)
    ]
    far_pre = [
        merge(one, two) for one, two in zip(exchange([first_pre] * len(others), [0]), far_pre)
    ]
    upstream = merge(first_up, upstream)
    grad_pre = merge(first_pre, grad_pre)
    far_states_out = [
        jnp.where(section_id < len(late), one, two)
        for one, two in zip(far_late, far_states_out)
    ]
    far_states = {0: far_states_in, 2: far_states_out}

    def far_part(e, which):
        size = size_out if which & 2 else size_in
        both = from_panels(far_states[which & 2][e - 1], size)
        half = both.shape[1] // 2
        return both[:, half:] if which & 1 else both[:, :half]

    def as_delta(left, right, scale):
        return (inner_rate * (dot(left, right, contract_rows) * scale)).astype(jnp.bfloat16)

    def finish(weight, moment, left, right, which, far_left, far_right, scale, pieces, size):
        new_weight, new_moment = outer_mix(
            weight.astype(jnp.float32),
            moment.astype(jnp.float32),
            as_delta(left, right, scale).astype(jnp.float32),
        )
        for e in others:
            back = replicas - e

            def mean(own_array, far_array):
                return 0.5 * (own_array.astype(jnp.float32) + far_array.astype(jnp.float32))

            index = pieces[back]
            own_left = piece(left, index, size, 1)
            part_weight, part_moment = outer_mix(
                mean(piece(weight, index, size), far_part(e, which)),
                mean(piece(moment, index, size), far_part(e, which + 1)),
                mean(
                    as_delta(own_left, right, scale),
                    as_delta(far_left[e - 1], far_right[e - 1], scale),
                ),
            )
            new_weight = lax.dynamic_update_slice_in_dim(new_weight, part_weight, index * size, 0)
            new_moment = lax.dynamic_update_slice_in_dim(new_moment, part_moment, index * size, 0)
        return new_weight[None, None], new_moment[None, None]

    new_weight_b, new_moment_b = finish(
        weight_out, moment_b[0, 0], hidden, upstream, 2, far_hidden, far_up,
        scale_out, pieces_out, size_out,
    )
    new_weight_a, new_moment_a = finish(
        weight_in, moment_a[0, 0], normed, grad_pre, 0, far_normed, far_pre,
        scale_in, pieces_in, size_in,
    )
    return (new_weight_a, new_weight_b, new_moment_a, new_moment_b)


def solution(mesh):
    placed = (
        P("replica", None, None, "shard"),
        P("replica", None, None, "shard"),
        P("replica", "section", None, "shard"),
        P("replica", "section", "shard", None),
        P("replica", "section", None, "shard"),
        P("replica", "section", "shard", None),
        P(),
        P(),
    )
    return jax.shard_map(
        per_device,
        mesh=mesh,
        in_specs=placed,
        out_specs=(
            P("replica", "section", None, "shard"),
            P("replica", "section", "shard", None),
            P("replica", "section", None, "shard"),
            P("replica", "section", "shard", None),
        ),
        check_vma=False,
    )
```

time: 212 us -> 225 us (1.061)
  the two profiles are of different devices: /device:TPU:0 before, /device:TPU:24 now
where the time goes in v1:
time: 225 us; the launch traced here: 224 us
  waiting for transfers between devices  115 us (51%)
  starting transfers between devices  51.2 us (23%)
  local copies, waits for them, and re-layouts  25.7 us (11%)
  Pallas kernels  15.7 us (7%)
  matrix products  7.14 us (3%)
  other arithmetic  4.75 us (2%)
  between operations  4.19 us (2%)
    ppermute x39, waiting for transfers between devices, move(): return lax.ppermute(array, axes, pairs)  115 us
    ppermute x39, starting transfers between devices, move(): return lax.ppermute(array, axes, pairs)  51.2 us
    unnamed x68, local copies, waits for them, and re-layouts  23.2 us
    pallas_call x7, Pallas kernels, chain_step(): pl.pallas_call(functools.partial(chain_kernel, sz, step, forward, (len(re...  9.78 us
    dot_general x9, matrix products, dot(): lax.dot_general(left, right, dims, preferred_element_type=jnp.float32)  7.14 us
    pallas_call x3, Pallas kernels, pack(): pl.pallas_call(functools.partial(pack_kernel, heights, panel), out_shape=...  5.97 us
  transfers between devices with their start and end apart: 39, of which 10 were waited for; matrix products, arithmetic and copies ran while one was open for 6% of the time, Pallas kernels for 3%

profile of v1, /device:TPU:24, one launch (start us, length us, event | category | flops | bytes accessed | tf_op | source)
XLA Modules:
  0.0 223.8 jit_solution(18139738723275939430)
XLA Ops:
  2.9 1.4 copy-done.17
  4.3 2.0 shard_map.111.refs_3_.refs_5_
  7.7 2.2 %collective-permute-start = (bf16[128,256]{1,0:T(8,128)(2,1)S(1)}, bf16[128,256]{1,0:T(8,128)(2,1)S(1)}, u32[]{:S(2)}, u32[]{:S(2)}) collective-permute-start(bf16[128,256]{1,0:T(8,128)(2,1)S(1)} %select_bitcast_fusion.refs_2_), channel_id=1, source_target_pairs={{3,1},{1,3},{15,13},{13,15},{19,17},{17,19},{31,29},{29,31}} | collective-permute-start | bytes 196616 | tf_op jit(solution)/shard_map/ppermute | solution.py:322
  11.6 3.3 %collective-permute-done.refs_1_.refs_3_ = bf16[128,256]{1,0:T(8,128)(2,1)S(1)} collective-permute-done((bf16[128,256]{1,0:T(8,128)(2,1)S(1)}, bf16[128,256]{1,0:T(8,128)(2,1)S(1)}, u32[]{:S(2)}, u32[]{:S(2)}) %collective-permute-start) | collective-permute-done | bytes 65568 | tf_op jit(solution)/shard_map/ppermute | solution.py:322
  14.9 32.0 %collective-permute-done.1.refs_2_.refs_4_ = bf16[128,256]{1,0:T(8,128)(2,1)S(1)} collective-permute-done((bf16[128,256]{1,0:T(8,128)(2,1)S(1)}, bf16[128,256]{1,0:T(8,128)(2,1)S(1)}, u32[]{:S(2)}, u32[]{:S(2)}) %collective-permute-start.1) | collective-permute-done | bytes 65568 | tf_op jit(solution)/shard_map/ppermute | solution.py:322
  48.8 5.0 %shard_map.112 = (bf16[64,1024]{1,0:T(8,128)(2,1)}, bf16[64,1024]{1,0:T(8,128)(2,1)}, bf16[128,1024]{1,0:T(8,128)(2,1)S(1)}, bf16[128,1024]{1,0:T(8,128)(2,1)S(1)}, f32[128,1536]{1,0:T(8,128)S(1)}) custom-call(s32[6,4]{1,0:T(8,128)S(1)} %fusion.38.refs_0_, ...), custom_call_target="tpu_custom_call", output_to_operand_aliasing={{2}: (5, {}), {3}: (6, {}), {4}: (7, {})} | custom-call | flops 805306368 | bytes 6291456 | tf_op jit(solution)/shard_map/pallas_call | solution.py:252
  55.4 1.9 collective-permute-start.3
  57.3 1.9 collective-permute-start.4
  59.3 1.9 collective-permute-start.5
  61.2 1.9 collective-permute-start.6
  77.7 1.4 copy-done.22
  79.1 2.0 shard_map.114
  92.6 1.9 shard_map.120
  94.6 1.6 collective-permute-start.30
  103.3 1.8 collective-permute-start.35
  114.2 52.0 %collective-permute-done.25 = bf16[64,1024]{1,0:T(8,128)(2,1)S(1)} collective-permute-done((bf16[64,1024]{1,0:T(8,128)(2,1)}, bf16[64,1024]{1,0:T(8,128)(2,1)S(1)}, u32[]{:S(2)}, u32[]{:S(2)}) %collective-permute-start.25) | collective-permute-done | bytes 131104 | tf_op jit(solution)/shard_map/ppermute | solution.py:322
  167.5 2.6 %collective-permute-done.27 = bf16[64,1024]{1,0:T(8,128)(2,1)S(1)} collective-permute-done((bf16[64,1024]{1,0:T(8,128)(2,1)}, bf16[64,1024]{1,0:T(8,128)(2,1)S(1)}, u32[]{:S(2)}, u32[]{:S(2)}) %collective-permute-start.27) | collective-permute-done | bytes 131104 | tf_op jit(solution)/shard_map/ppermute | solution.py:322
  172.2 3.2 %collective-permute-done.28 = bf16[64,1024]{1,0:T(8,128)(2,1)S(1)} collective-permute-done((bf16[64,1024]{1,0:T(8,128)(2,1)}, bf16[64,1024]{1,0:T(8,128)(2,1)S(1)}, u32[]{:S(2)}, u32[]{:S(2)}) %collective-permute-start.28) | collective-permute-done | bytes 131104 | tf_op jit(solution)/shard_map/ppermute | solution.py:322
  176.9 1.5 fusion.50
  178.4 3.2 %collective-permute-start.34 = (bf16[3072,256]{1,0:T(8,128)(2,1)}, bf16[3072,256]{1,0:T(8,128)(2,1)S(1)}, u32[]{:S(2)}, u32[]{:S(2)}) collective-permute-start(bf16[3072,256]{1,0:T(8,128)(2,1)} %shard_map.114), channel_id=1, source_target_pairs={{0,16},{1,17},{2,18},{3,19},{4,20},{5,21},{6,22},{7,23},{16,0},{17... | collective-permute-start | bytes 4718600 | tf_op jit(solution)/shard_map/ppermute | solution.py:322
  187.0 2.9 %collective-permute-start.32 = (bf16[128,768]{1,0:T(8,128)(2,1)S(1)}, bf16[128,768]{1,0:T(8,128)(2,1)S(1)}, u32[]{:S(2)}, u32[]{:S(2)}) collective-permute-start(bf16[128,768]{1,0:T(8,128)(2,1)S(1)} %fusion.26), channel_id=1, source_target_pairs={{0,16},{1,17},{2,18},{3,19},{16,0},{17,1},{18,2},{19,3}} | collective-permute-start | bytes 589832 | tf_op jit(solution)/shard_map/ppermute | solution.py:322
  194.1 17.7 %collective-permute-done.31 = bf16[128,512]{1,0:T(8,128)(2,1)S(1)} collective-permute-done((bf16[128,512]{1,0:T(8,128)(2,1)S(1)}, bf16[128,512]{1,0:T(8,128)(2,1)S(1)}, u32[]{:S(2)}, u32[]{:S(2)}) %collective-permute-start.31) | collective-permute-done | bytes 131104 | tf_op jit(solution)/shard_map/ppermute | solution.py:322
  211.8 3.2 %collective-permute-start.37 = (bf16[128,1024]{1,0:T(8,128)(2,1)S(1)}, bf16[128,1024]{1,0:T(8,128)(2,1)S(1)}, u32[]{:S(2)}, u32[]{:S(2)}) collective-permute-start(bf16[128,1024]{1,0:T(8,128)(2,1)S(1)} %broadcast_select_fusion.3), channel_id=1, source_target_pairs={{0,16},{1,17},{2,18},{3,19},{16,0},{17,1},{18,2},{19,3}} | collective-permute-start | bytes 786440 | tf_op jit(solution)/shard_map/ppermute | solution.py:322
  219.3 1.7 collective-permute-done.36
  (180 shorter events, 69.2 us)
Async XLA Ops:
  6.4 41.4 %collective-permute-start.2 = (bf16[6272,256]{1,0:T(8,128)(2,1)S(1)}, bf16[6272,256]{1,0:T(8,128)(2,1)}, u32[]{:S(2)}, u32[]{:S(2)}) collective-permute-start(bf16[6272,256]{1,0:T(8,128)(2,1)S(1)} %shard_map.111.refs_3_.refs_5_), channel_id=1, source_target_pairs={{0,1},{2,3},{5,4},{7,6},{9,8},{11,10},{12,13},{14,15},{16,17},{18,... | collective-permute-start | bytes 9633800 | tf_op jit(solution)/shard_map/ppermute | solution.py:322
  7.7 7.2 %collective-permute-start = (bf16[128,256]{1,0:T(8,128)(2,1)S(1)}, bf16[128,256]{1,0:T(8,128)(2,1)S(1)}, u32[]{:S(2)}, u32[]{:S(2)}) collective-permute-start(bf16[128,256]{1,0:T(8,128)(2,1)S(1)} %select_bitcast_fusion.refs_2_), channel_id=1, source_target_pairs={{3,1},{1,3},{15,13},{13,15},{19,17},{17,19},{31,29},{29,31}} | collective-permute-start | bytes 196616 | tf_op jit(solution)/shard_map/ppermute | solution.py:322
  10.0 36.9 %collective-permute-start.1 = (bf16[128,256]{1,0:T(8,128)(2,1)S(1)}, bf16[128,256]{1,0:T(8,128)(2,1)S(1)}, u32[]{:S(2)}, u32[]{:S(2)}) collective-permute-start(bf16[128,256]{1,0:T(8,128)(2,1)S(1)} %select_bitcast_fusion.refs_2_), channel_id=1, source_target_pairs={{2,1},{0,3},{14,13},{12,15},{18,17},{16,19},{30,29},{28,31}} | collective-permute-start | bytes 196616 | tf_op jit(solution)/shard_map/ppermute | solution.py:322
  55.4 8.6 %collective-permute-start.3 = (bf16[64,1024]{1,0:T(8,128)(2,1)}, bf16[64,1024]{1,0:T(8,128)(2,1)}, u32[]{:S(2)}, u32[]{:S(2)}) collective-permute-start(bf16[64,1024]{1,0:T(8,128)(2,1)} %get-tuple-element.45), channel_id=1, source_target_pairs={{1,4},{3,6},{17,20},{19,22}} | collective-permute-start | bytes 393224 | tf_op jit(solution)/shard_map/ppermute | solution.py:322
  57.3 6.6 %collective-permute-start.4 = (bf16[64,1024]{1,0:T(8,128)(2,1)}, bf16[64,1024]{1,0:T(8,128)(2,1)}, u32[]{:S(2)}, u32[]{:S(2)}) collective-permute-start(bf16[64,1024]{1,0:T(8,128)(2,1)} %get-tuple-element.45), channel_id=1, source_target_pairs={{1,6},{3,4},{17,22},{19,20}} | collective-permute-start | bytes 393224 | tf_op jit(solution)/shard_map/ppermute | solution.py:322
  69.8 11.4 %collective-permute-start.7 = (bf16[64,1024]{1,0:T(8,128)(2,1)}, bf16[64,1024]{1,0:T(8,128)(2,1)}, u32[]{:S(2)}, u32[]{:S(2)}) collective-permute-start(bf16[64,1024]{1,0:T(8,128)(2,1)} %get-tuple-element.50), channel_id=1, source_target_pairs={{4,8},{6,10},{20,24},{22,26}} | collective-permute-start | bytes 393224 | tf_op jit(solution)/shard_map/ppermute | solution.py:322
  71.1 10.1 %collective-permute-start.8 = (bf16[64,1024]{1,0:T(8,128)(2,1)}, bf16[64,1024]{1,0:T(8,128)(2,1)}, u32[]{:S(2)}, u32[]{:S(2)}) collective-permute-start(bf16[64,1024]{1,0:T(8,128)(2,1)} %get-tuple-element.50), channel_id=1, source_target_pairs={{4,10},{6,8},{20,26},{22,24}} | collective-permute-start | bytes 393224 | tf_op jit(solution)/shard_map/ppermute | solution.py:322
  72.4 8.8 %collective-permute-start.10 = (bf16[64,1024]{1,0:T(8,128)(2,1)}, bf16[64,1024]{1,0:T(8,128)(2,1)}, u32[]{:S(2)}, u32[]{:S(2)}) collective-permute-start(bf16[64,1024]{1,0:T(8,128)(2,1)} %get-tuple-element.51), channel_id=1, source_target_pairs={{4,26},{6,24},{20,10},{22,8}} | collective-permute-start | bytes 393224 | tf_op jit(solution)/shard_map/ppermute | solution.py:322
  73.7 7.5 %collective-permute-start.9 = (bf16[64,1024]{1,0:T(8,128)(2,1)}, bf16[64,1024]{1,0:T(8,128)(2,1)}, u32[]{:S(2)}, u32[]{:S(2)}) collective-permute-start(bf16[64,1024]{1,0:T(8,128)(2,1)} %get-tuple-element.51), channel_id=1, source_target_pairs={{4,24},{6,26},{20,8},{22,10}} | collective-permute-start | bytes 393224 | tf_op jit(solution)/shard_map/ppermute | solution.py:322
  87.1 9.0 %collective-permute-start.15 = (bf16[128,1024]{1,0:T(8,128)(2,1)}, bf16[128,1024]{1,0:T(8,128)(2,1)}, u32[]{:S(2)}, u32[]{:S(2)}) collective-permute-start(bf16[128,1024]{1,0:T(8,128)(2,1)} %get-tuple-element.65.refs_1_), channel_id=1, source_target_pairs={{13,15},{15,13},{29,31},{31,29}} | collective-permute-start | bytes 786440 | tf_op jit(solution)/shard_map/ppermute | solution.py:322
  94.6 82.3 %collective-permute-start.30 = (bf16[3072,256]{1,0:T(8,128)(2,1)}, bf16[3072,256]{1,0:T(8,128)(2,1)}, u32[]{:S(2)}, u32[]{:S(2)}) collective-permute-start(bf16[3072,256]{1,0:T(8,128)(2,1)} %shard_map.120), channel_id=1, source_target_pairs={{0,16},{1,17},{2,18},{3,19},{4,20},{5,21},{6,22},{7,23},{8,24},{9,... | collective-permute-start | bytes 4718600 | tf_op jit(solution)/shard_map/ppermute | solution.py:322
  103.3 114.3 %collective-permute-start.35 = (bf16[3072,256]{1,0:T(8,128)(2,1)}, bf16[3072,256]{1,0:T(8,128)(2,1)}, u32[]{:S(2)}, u32[]{:S(2)}) collective-permute-start(bf16[3072,256]{1,0:T(8,128)(2,1)} %shard_map.114), channel_id=1, source_target_pairs={{8,24},{9,25},{10,26},{11,27},{12,28},{13,29},{14,30},{15,31},{24,... | collective-permute-start | bytes 4718600 | tf_op jit(solution)/shard_map/ppermute | solution.py:322
  107.3 58.9 %collective-permute-start.25 = (bf16[64,1024]{1,0:T(8,128)(2,1)}, bf16[64,1024]{1,0:T(8,128)(2,1)S(1)}, u32[]{:S(2)}, u32[]{:S(2)}) collective-permute-start(bf16[64,1024]{1,0:T(8,128)(2,1)} %get-tuple-element.81), channel_id=1, source_target_pairs={{4,1},{6,3},{20,17},{22,19}} | collective-permute-start | bytes 393224 | tf_op jit(solution)/shard_map/ppermute | solution.py:322
  110.5 59.6 %collective-permute-start.27 = (bf16[64,1024]{1,0:T(8,128)(2,1)}, bf16[64,1024]{1,0:T(8,128)(2,1)S(1)}, u32[]{:S(2)}, u32[]{:S(2)}) collective-permute-start(bf16[64,1024]{1,0:T(8,128)(2,1)} %get-tuple-element.81), channel_id=1, source_target_pairs={{4,3},{6,1},{20,19},{22,17}} | collective-permute-start | bytes 393224 | tf_op jit(solution)/shard_map/ppermute | solution.py:322
  111.8 60.4 %collective-permute-start.26 = (bf16[64,1024]{1,0:T(8,128)(2,1)}, bf16[64,1024]{1,0:T(8,128)(2,1)S(1)}, u32[]{:S(2)}, u32[]{:S(2)}) collective-permute-start(bf16[64,1024]{1,0:T(8,128)(2,1)} %copy-done.27), channel_id=1, source_target_pairs={{4,17},{6,19},{20,1},{22,3}} | collective-permute-start | bytes 393224 | tf_op jit(solution)/shard_map/ppermute | solution.py:322
  166.2 9.3 %collective-permute-start.28 = (bf16[64,1024]{1,0:T(8,128)(2,1)}, bf16[64,1024]{1,0:T(8,128)(2,1)S(1)}, u32[]{:S(2)}, u32[]{:S(2)}) collective-permute-start(bf16[64,1024]{1,0:T(8,128)(2,1)} %copy-done.27), channel_id=1, source_target_pairs={{4,19},{6,17},{20,3},{22,1}} | collective-permute-start | bytes 393224 | tf_op jit(solution)/shard_map/ppermute | solution.py:322
  170.1 11.5 %collective-permute-start.24 = (bf16[256,1024]{1,0:T(8,128)(2,1)S(1)}, bf16[256,1024]{1,0:T(8,128)(2,1)S(1)}, u32[]{:S(2)}, u32[]{:S(2)}) collective-permute-start(bf16[256,1024]{1,0:T(8,128)(2,1)S(1)} %pad_maximum_fusion.2), channel_id=1, source_target_pairs={{1,0},{3,2},{4,5},{6,7},{8,9},{10,11},{13,12},{15,14},{17,16},{19,... | collective-permute-start | bytes 1572872 | tf_op jit(solution)/shard_map/ppermute | solution.py:322
  175.6 6.0 %collective-permute-start.29 = (bf16[128,1024]{1,0:T(8,128)(2,1)S(1)}, bf16[128,1024]{1,0:T(8,128)(2,1)S(1)}, u32[]{:S(2)}, u32[]{:S(2)}) collective-permute-start(bf16[128,1024]{1,0:T(8,128)(2,1)S(1)} %add_convert_fusion), channel_id=1, source_target_pairs={{1,0},{3,2},{17,16},{19,18}} | collective-permute-start | bytes 786440 | tf_op jit(solution)/shard_map/ppermute | solution.py:322
  178.4 39.2 %collective-permute-start.34 = (bf16[3072,256]{1,0:T(8,128)(2,1)}, bf16[3072,256]{1,0:T(8,128)(2,1)S(1)}, u32[]{:S(2)}, u32[]{:S(2)}) collective-permute-start(bf16[3072,256]{1,0:T(8,128)(2,1)} %shard_map.114), channel_id=1, source_target_pairs={{0,16},{1,17},{2,18},{3,19},{4,20},{5,21},{6,22},{7,23},{16,0},{17... | collective-permute-start | bytes 4718600 | tf_op jit(solution)/shard_map/ppermute | solution.py:322
  186.2 28.8 %collective-permute-start.33 = (bf16[128,768]{1,0:T(8,128)(2,1)S(1)}, bf16[128,768]{1,0:T(8,128)(2,1)S(1)}, u32[]{:S(2)}, u32[]{:S(2)}) collective-permute-start(bf16[128,768]{1,0:T(8,128)(2,1)S(1)} %fusion.27), channel_id=1, source_target_pairs={{4,20},{5,21},{6,22},{7,23},{8,24},{9,25},{10,26},{11,27},{12,28},... | collective-permute-start | bytes 589832 | tf_op jit(solution)/shard_map/ppermute | solution.py:322
  187.0 28.8 %collective-permute-start.32 = (bf16[128,768]{1,0:T(8,128)(2,1)S(1)}, bf16[128,768]{1,0:T(8,128)(2,1)S(1)}, u32[]{:S(2)}, u32[]{:S(2)}) collective-permute-start(bf16[128,768]{1,0:T(8,128)(2,1)S(1)} %fusion.26), channel_id=1, source_target_pairs={{0,16},{1,17},{2,18},{3,19},{16,0},{17,1},{18,2},{19,3}} | collective-permute-start | bytes 589832 | tf_op jit(solution)/shard_map/ppermute | solution.py:322
  189.9 21.8 %collective-permute-start.31 = (bf16[128,512]{1,0:T(8,128)(2,1)S(1)}, bf16[128,512]{1,0:T(8,128)(2,1)S(1)}, u32[]{:S(2)}, u32[]{:S(2)}) collective-permute-start(bf16[128,512]{1,0:T(8,128)(2,1)S(1)} %constant_dynamic-slice_fusion.1), channel_id=1, source_target_pairs={{0,16},{1,17},{2,18},{3,19},{4,20},{5,21},{6,22},{7,23},{8,24},{9,... | collective-permute-start | bytes 393224 | tf_op jit(solution)/shard_map/ppermute | solution.py:322
  211.8 9.3 %collective-permute-start.37 = (bf16[128,1024]{1,0:T(8,128)(2,1)S(1)}, bf16[128,1024]{1,0:T(8,128)(2,1)S(1)}, u32[]{:S(2)}, u32[]{:S(2)}) collective-permute-start(bf16[128,1024]{1,0:T(8,128)(2,1)S(1)} %broadcast_select_fusion.3), channel_id=1, source_target_pairs={{0,16},{1,17},{2,18},{3,19},{16,0},{17,1},{18,2},{19,3}} | collective-permute-start | bytes 786440 | tf_op jit(solution)/shard_map/ppermute | solution.py:322
  214.9 6.1 %collective-permute-start.36 = (bf16[128,384]{1,0:T(8,128)(2,1)S(1)}, bf16[128,384]{1,0:T(8,128)(2,1)S(1)}, u32[]{:S(2)}, u32[]{:S(2)}) collective-permute-start(bf16[128,384]{1,0:T(8,128)(2,1)S(1)} %constant_dynamic-slice_fusion), channel_id=1, source_target_pairs={{0,16},{1,17},{2,18},{3,19},{4,20},{5,21},{6,22},{7,23},{8,24},{9,... | collective-permute-start | bytes 294920 | tf_op jit(solution)/shard_map/ppermute | solution.py:322
  (49 other events, 118.1 us)

commit v2 on v1

--- a/solution.py
+++ b/solution.py
@@ -114,10 +114,10 @@
 
     (table,) = take(1)
     received, edges, payloads = take(counts[0]), take(counts[1]), take(2)
-    take(3)
+    take(1)
     sends = take(counts[2])
-    rows_hbm, up_hbm, slope_hbm = take(3)
-    weights, landing, rows, up, out, slope = take(6)
+    (state,) = take(1)
+    weights, landing, rows, up, out, slope, wide_store = take(7)
     weight_sems, block_sems, edge_sems, send_sems, state_sems = take(5)
     panel, width, hidden_size = sz.panel, sz.width, sz.local_hidden
     links = sz.sections - 1
@@ -132,6 +132,12 @@
 
     def place(line, e):
         return pl.ds(pl.multiple_of(table[line, e], sz.block_rows), sz.block_rows)
+
+    def state_part(k, columns):
+        return state.at[pl.ds(k * sz.row_count, sz.row_count), pl.ds(0, columns)]
+
+    rows_hbm, up_hbm = state_part(0, width), state_part(1, width)
+    slope_hbm = state_part(2, 2 * hidden_size)
 
     @pl.when(table[links + 1, step] == 1)
     def _():
@@ -152,7 +158,7 @@
                     pltpu.make_async_copy(source, out.at[:, column], edge_sems.at[d])
                 )
         if not forward:
-            first_copies.append(pltpu.make_async_copy(rows_hbm, rows, state_sems.at[0]))
+            first_copies.append(pltpu.make_async_copy(rows_hbm, wide_store, state_sems.at[0]))
             first_copies.append(pltpu.make_async_copy(slope_hbm, slope, state_sems.at[1]))
         for copy in first_copies:
             copy.start()
@@ -177,11 +183,14 @@
             up[...] = (total.astype(jnp.float32) - goal).astype(jnp.bfloat16)
         else:
             up[...] = total
-        fresh, fresh_hbm = (rows, rows_hbm) if forward else (up, up_hbm)
-        store_copies = [pltpu.make_async_copy(fresh, fresh_hbm, state_sems.at[2])]
-        store_copies[0].start()
-
-        wide = rows[...].astype(jnp.float32)
+        if forward:
+            wide = rows[...].astype(jnp.float32)
+            wide_store[...] = wide
+            store_copies = [pltpu.make_async_copy(wide_store, rows_hbm, state_sems.at[2])]
+        else:
+            wide = wide_store[...]
+            up_store = slope.at[:, pl.ds(0, width)]
+            store_copies = [pltpu.make_async_copy(up_store, up_hbm, state_sems.at[2])]
         inverse_rms = lax.rsqrt(jnp.mean(wide * wide, axis=1, keepdims=True) + epsilon)
         leads = table[links + 2, 2] > table[links + 2, 0]
         if forward:
@@ -225,7 +234,9 @@
             total = total.T * sz.scale_in
             exact = wide * inverse_rms
             along = jnp.mean(total * exact, axis=1, keepdims=True)
-            own = jnp.where(leads, up[...].astype(jnp.float32), 0.0)
+            own = up[...].astype(jnp.float32)
+            slope[:, :width] = own
+            own = jnp.where(leads, own, 0.0)
             out[...] = (own + inverse_rms * (total - exact * along)).astype(jnp.bfloat16)
         leave = step if forward else links
         send_copies = []
@@ -234,20 +245,19 @@
             send_copies.append(
                 pltpu.make_async_copy(out.at[rows_here], target, send_sems.at[e])
             )
-        for copy in send_copies + store_copies[1:]:
+        for copy in send_copies + store_copies:
             copy.start()
         for copy in send_copies + store_copies:
             copy.wait()
 
 
-def chain_step(sz, step, forward, table, received, edges, payloads, states):
+def chain_step(sz, step, forward, table, received, edges, payloads, state):
     last = step + 1 == sz.sections
     count = 1 if forward and last else sz.blocks
     anywhere = pl.BlockSpec(memory_space=pl.ANY)
-    operands = [table, *received, *edges, *payloads, *states]
+    operands = [table, *received, *edges, *payloads, state]
     block = jax.ShapeDtypeStruct((sz.row_count // count, sz.width), jnp.bfloat16)
-    shapes = [block] * count + [jax.ShapeDtypeStruct(s.shape, s.dtype) for s in states]
-    base = len(operands) - len(states)
+    shapes = [block] * count + [jax.ShapeDtypeStruct(state.shape, state.dtype)]
     whole = (sz.row_count, sz.width)
     results = pl.pallas_call(
         functools.partial(
@@ -256,7 +266,7 @@
         out_shape=shapes,
         in_specs=[pl.BlockSpec(memory_space=pltpu.SMEM)] + [anywhere] * (len(operands) - 1),
         out_specs=[anywhere] * len(shapes),
-        input_output_aliases={base + i: count + i for i in range(len(states))},
+        input_output_aliases={len(operands) - 1: count},
         scratch_shapes=[
             pltpu.VMEM((2, 2, sz.half, sz.panel), jnp.bfloat16),
             pltpu.VMEM((2,) + whole, jnp.bfloat16),
@@ -264,6 +274,7 @@
             pltpu.VMEM(whole, jnp.bfloat16),
             pltpu.VMEM(whole, jnp.bfloat16),
             pltpu.VMEM((sz.row_count, 2 * sz.local_hidden), jnp.float32),
+            pltpu.VMEM(whole, jnp.float32),
             pltpu.SemaphoreType.DMA((2, 2)),
             pltpu.SemaphoreType.DMA((max(1, len(received)),)),
             pltpu.SemaphoreType.DMA((4,)),
@@ -277,7 +288,7 @@
             transcendentals=0,
         ),
     )(*operands)
-    return list(results[:count]), list(results[count:])
+    return list(results[:count]), results[count]
 
 
 def per_device(inputs, targets, weight_a, weight_b, moment_a, moment_b, routes, partners):
@@ -429,15 +440,11 @@
                 moved[a] = lax.dynamic_update_index_in_dim(moved[a], got, arrived[e], 0)
         return [one.reshape(row_count, width) for one in moved]
 
-    states = [
-        jnp.zeros((row_count, width), jnp.bfloat16),
-        jnp.zeros((row_count, width), jnp.bfloat16),
-        jnp.zeros((row_count, 2 * local_hidden), jnp.float32),
-    ]
+    state = jnp.zeros((5 * row_count, 2 * local_hidden), jnp.float32)
     received = []
     for step in every:
-        sends, states = chain_step(
-            sz, step, True, table, received, edges if step == 0 else [], payloads, states
+        sends, state = chain_step(
+            sz, step, True, table, received, edges if step == 0 else [], payloads, state
         )
         if step < links:
             received = send_blocks(sends, back, slots[step], step, 1)
@@ -446,14 +453,20 @@
         if step == len(late) - 1:
             received, packed_out = lax.optimization_barrier((received, packed_out))
             far_late = exchange(packed_out, late)
+        if step == len(late):
+            received, far_states_in, far_states_out = lax.optimization_barrier(
+                (received, far_states_in, far_states_out)
+            )
 
     for step in reversed(range(1, sections)):
-        sends, states = chain_step(
-            sz, step, False, table, received, edges if step == links else [], payloads, states
+        sends, state = chain_step(
+            sz, step, False, table, received, edges if step == links else [], payloads, state
         )
         received = send_blocks(sends, slots[step - 1], back, step, -1)
-
-    known, sends = lax.optimization_barrier((jnp.concatenate(states[:2]), sends))
+        if step == len(late):
+            received, far_late = lax.optimization_barrier((received, far_late))
+
+    known = state[: 2 * row_count, :width].astype(jnp.bfloat16)
     known = jnp.where(is_holder, known, from_holders(known, 1, every))
     own_rows, upstream = known[:row_count], known[row_count:]
     inverse_rms = norm_scale(own_rows)

time: 225 us -> 217 us (0.964)
  the two profiles are of different devices: /device:TPU:24 before, /device:TPU:4 now
where the time goes in v2:
time: 217 us; the launch traced here: 216 us
  waiting for transfers between devices  91.6 us (42%)
  starting transfers between devices  69.2 us (32%)
  Pallas kernels  21.3 us (10%)
  local copies, waits for them, and re-layouts  18.4 us (8%)
  matrix products  7.15 us (3%)
  other arithmetic  4.6 us (2%)
  between operations  4.2 us (2%)
    ppermute x39, waiting for transfers between devices, move(): return lax.ppermute(array, axes, pairs)  91.6 us
    ppermute x39, starting transfers between devices, move(): return lax.ppermute(array, axes, pairs)  69.2 us
    unnamed x36, local copies, waits for them, and re-layouts  15.5 us
    pallas_call x7, Pallas kernels, chain_step(): pl.pallas_call(functools.partial(chain_kernel, sz, step, forward, (len(re...  15.4 us
    dot_general x9, matrix products, dot(): lax.dot_general(left, right, dims, preferred_element_type=jnp.float32)  7.15 us
    pallas_call x3, Pallas kernels, pack(): pl.pallas_call(functools.partial(pack_kernel, heights, panel), out_shape=...  5.97 us
  transfers between devices with their start and end apart: 39, of which 14 were waited for; matrix products, arithmetic and copies ran while one was open for 6% of the time, Pallas kernels for 9%

profile of v2, /device:TPU:4, one launch (start us, length us, event | category | flops | bytes accessed | tf_op | source)
XLA Modules:
  0.0 216.4 jit_solution(3842091119162852946)
XLA Ops:
  4.4 2.0 shard_map.111.refs_3_.refs_5_
  13.5 1.9 shard_map.116
  15.4 1.6 collective-permute-start.15
  21.0 2.0 shard_map.114
  23.1 2.4 %collective-permute-start.16 = (bf16[3072,256]{1,0:T(8,128)(2,1)}, bf16[3072,256]{1,0:T(8,128)(2,1)}, u32[]{:S(2)}, u32[]{:S(2)}) collective-permute-start(bf16[3072,256]{1,0:T(8,128)(2,1)} %shard_map.114), channel_id=1, source_target_pairs={{8,24},{9,25},{10,26},{11,27},{12,28},{13,29},{14,30},{15,31},{24,... | collective-permute-start | bytes 4718600 | tf_op jit(solution)/shard_map/ppermute | solution.py:333
  25.8 20.5 %collective-permute-done.2.refs_4_.refs_6_ = bf16[6272,256]{1,0:T(8,128)(2,1)} collective-permute-done((bf16[6272,256]{1,0:T(8,128)(2,1)S(1)}, bf16[6272,256]{1,0:T(8,128)(2,1)}, u32[]{:S(2)}, u32[]{:S(2)}) %collective-permute-start.2) | collective-permute-done | bytes 3211296 | tf_op jit(solution)/shard_map/ppermute | solution.py:333
  55.0 22.9 %collective-permute-done.10.refs_4_ = bf16[64,1024]{1,0:T(8,128)(2,1)S(1)} collective-permute-done((bf16[64,1024]{1,0:T(8,128)(2,1)S(1)}, bf16[64,1024]{1,0:T(8,128)(2,1)S(1)}, u32[]{:S(2)}, u32[]{:S(2)}) %collective-permute-start.10) | collective-permute-done | bytes 131104 | tf_op jit(solution)/shard_map/ppermute | solution.py:333
  79.5 5.6 %collective-permute-done.9.refs_3_ = bf16[64,1024]{1,0:T(8,128)(2,1)S(1)} collective-permute-done((bf16[64,1024]{1,0:T(8,128)(2,1)S(1)}, bf16[64,1024]{1,0:T(8,128)(2,1)S(1)}, u32[]{:S(2)}, u32[]{:S(2)}) %collective-permute-start.9) | collective-permute-done | bytes 131104 | tf_op jit(solution)/shard_map/ppermute | solution.py:333
  85.1 1.9 collective-permute-start.26
  87.0 4.9 %shard_map.115 = (bf16[64,1024]{1,0:T(8,128)(2,1)S(1)}, bf16[64,1024]{1,0:T(8,128)(2,1)S(1)}, f32[640,1536]{1,0:T(8,128)S(1)}) custom-call(s32[6,4]{1,0:T(8,128)S(1)} %fusion.38.refs_0_, bf16[64,1024]{1,0:T(8,128)(2,1)S(1)} %collective-permute-done.7.refs_1_, bf16[64,1024]{1,0:T(8,128)(2,1)S(1)} %collective-permute-done.8.refs_2_, ...), custom_call_target="tpu_custom_call", output_to_operand_aliasing={{2}: (7, {})} | custom-call | flops 805306368 | bytes 6291456 | tf_op jit(solution)/shard_map/pallas_call | solution.py:262
  102.2 1.8 copy-done.1
  111.1 15.9 %collective-permute-done.18.refs_1_ = bf16[64,1024]{1,0:T(8,128)(2,1)S(1)} collective-permute-done((bf16[64,1024]{1,0:T(8,128)(2,1)}, bf16[64,1024]{1,0:T(8,128)(2,1)S(1)}, u32[]{:S(2)}, u32[]{:S(2)}) %collective-permute-start.18) | collective-permute-done | bytes 131104 | tf_op jit(solution)/shard_map/ppermute | solution.py:333
  127.0 3.3 %collective-permute-done.19.refs_2_ = bf16[64,1024]{1,0:T(8,128)(2,1)S(1)} collective-permute-done((bf16[64,1024]{1,0:T(8,128)(2,1)}, bf16[64,1024]{1,0:T(8,128)(2,1)S(1)}, u32[]{:S(2)}, u32[]{:S(2)}) %collective-permute-start.19) | collective-permute-done | bytes 131104 | tf_op jit(solution)/shard_map/ppermute | solution.py:333
  130.3 1.7 collective-permute-done.20.refs_3_
  132.0 2.3 %collective-permute-done.21.refs_4_ = bf16[64,1024]{1,0:T(8,128)(2,1)} collective-permute-done((bf16[64,1024]{1,0:T(8,128)(2,1)}, bf16[64,1024]{1,0:T(8,128)(2,1)}, u32[]{:S(2)}, u32[]{:S(2)}) %collective-permute-start.21) | collective-permute-done | bytes 131104 | tf_op jit(solution)/shard_map/ppermute | solution.py:333
  134.3 2.1 copy-done.2
  136.4 6.6 %shard_map.119 = (bf16[64,1024]{1,0:T(8,128)(2,1)S(1)}, bf16[64,1024]{1,0:T(8,128)(2,1)S(1)}, f32[640,1536]{1,0:T(8,128)S(1)}) custom-call(s32[6,4]{1,0:T(8,128)S(1)} %fusion.38.refs_0_, bf16[64,1024]{1,0:T(8,128)(2,1)S(1)} %collective-permute-done.18.refs_1_, bf16[64,1024]{1,0:T(8,128)(2,1)S(1)} %collective-permute-done.19.refs_2_, ...), custom_call_target="tpu_custom_call", output_to_operand_aliasing={{2}: (7, {})} | custom-call | flops 805306368 | bytes 6291456 | tf_op jit(solution)/shard_map/pallas_call | solution.py:262
  155.7 1.6 broadcast_select_fusion
  159.3 3.1 %collective-permute-done.27 = bf16[256,1024]{1,0:T(8,128)(2,1)S(1)} collective-permute-done((bf16[256,1024]{1,0:T(8,128)(2,1)S(1)}, bf16[256,1024]{1,0:T(8,128)(2,1)S(1)}, u32[]{:S(2)}, u32[]{:S(2)}) %collective-permute-start.27) | collective-permute-done | bytes 524320 | tf_op jit(solution)/shard_map/ppermute | solution.py:333
  166.3 19.3 %collective-permute-start.36 = (bf16[128,384]{1,0:T(8,128)(2,1)S(1)}, bf16[128,384]{1,0:T(8,128)(2,1)S(1)}, u32[]{:S(2)}, u32[]{:S(2)}) collective-permute-start(bf16[128,384]{1,0:T(8,128)(2,1)S(1)} %constant_dynamic-slice_fusion), channel_id=1, source_target_pairs={{0,16},{1,17},{2,18},{3,19},{4,20},{5,21},{6,22},{7,23},{8,24},{9,... | collective-permute-start | bytes 294920 | tf_op jit(solution)/shard_map/ppermute | solution.py:333
  187.0 3.6 %collective-permute-start.35 = (bf16[128,768]{1,0:T(8,128)(2,1)S(1)}, bf16[128,768]{1,0:T(8,128)(2,1)S(1)}, u32[]{:S(2)}, u32[]{:S(2)}) collective-permute-start(bf16[128,768]{1,0:T(8,128)(2,1)S(1)} %fusion.27), channel_id=1, source_target_pairs={{4,20},{5,21},{6,22},{7,23},{8,24},{9,25},{10,26},{11,27},{12,28},... | collective-permute-start | bytes 589832 | tf_op jit(solution)/shard_map/ppermute | solution.py:333
  193.5 5.1 %collective-permute-done.33 = bf16[128,512]{1,0:T(8,128)(2,1)S(1)} collective-permute-done((bf16[128,512]{1,0:T(8,128)(2,1)S(1)}, bf16[128,512]{1,0:T(8,128)(2,1)S(1)}, u32[]{:S(2)}, u32[]{:S(2)}) %collective-permute-start.33) | collective-permute-done | bytes 131104 | tf_op jit(solution)/shard_map/ppermute | solution.py:333
  198.6 7.0 %collective-permute-start.38 = (bf16[128,1024]{1,0:T(8,128)(2,1)S(1)}, bf16[128,1024]{1,0:T(8,128)(2,1)S(1)}, u32[]{:S(2)}, u32[]{:S(2)}) collective-permute-start(bf16[128,1024]{1,0:T(8,128)(2,1)S(1)} %slice.91), channel_id=1, source_target_pairs={{4,20},{5,21},{6,22},{7,23},{8,24},{9,25},{10,26},{11,27},{12,28},... | collective-permute-start | bytes 786440 | tf_op jit(solution)/shard_map/ppermute | solution.py:333
  206.8 6.9 %collective-permute-done.38 = bf16[128,1024]{1,0:T(8,128)(2,1)S(1)} collective-permute-done((bf16[128,1024]{1,0:T(8,128)(2,1)S(1)}, bf16[128,1024]{1,0:T(8,128)(2,1)S(1)}, u32[]{:S(2)}, u32[]{:S(2)}) %collective-permute-start.38) | collective-permute-done | bytes 262176 | tf_op jit(solution)/shard_map/ppermute | solution.py:333
  (146 shorter events, 66.1 us)
Async XLA Ops:
  6.4 40.0 %collective-permute-start.2 = (bf16[6272,256]{1,0:T(8,128)(2,1)S(1)}, bf16[6272,256]{1,0:T(8,128)(2,1)}, u32[]{:S(2)}, u32[]{:S(2)}) collective-permute-start(bf16[6272,256]{1,0:T(8,128)(2,1)S(1)} %shard_map.111.refs_3_.refs_5_), channel_id=1, source_target_pairs={{0,1},{2,3},{5,4},{7,6},{9,8},{11,10},{12,13},{14,15},{16,17},{18,... | collective-permute-start | bytes 9633800 | tf_op jit(solution)/shard_map/ppermute | solution.py:333
  7.7 18.1 %collective-permute-start = (bf16[128,256]{1,0:T(8,128)(2,1)S(1)}, bf16[128,256]{1,0:T(8,128)(2,1)S(1)}, u32[]{:S(2)}, u32[]{:S(2)}) collective-permute-start(bf16[128,256]{1,0:T(8,128)(2,1)S(1)} %select_bitcast_fusion.refs_2_), channel_id=1, source_target_pairs={{3,1},{1,3},{15,13},{13,15},{19,17},{17,19},{31,29},{29,31}} | collective-permute-start | bytes 196616 | tf_op jit(solution)/shard_map/ppermute | solution.py:333
  8.4 17.5 %collective-permute-start.1 = (bf16[128,256]{1,0:T(8,128)(2,1)S(1)}, bf16[128,256]{1,0:T(8,128)(2,1)S(1)}, u32[]{:S(2)}, u32[]{:S(2)}) collective-permute-start(bf16[128,256]{1,0:T(8,128)(2,1)S(1)} %select_bitcast_fusion.refs_2_), channel_id=1, source_target_pairs={{2,1},{0,3},{14,13},{12,15},{18,17},{16,19},{30,29},{28,31}} | collective-permute-start | bytes 196616 | tf_op jit(solution)/shard_map/ppermute | solution.py:333
  15.4 79.1 %collective-permute-start.15 = (bf16[3072,256]{1,0:T(8,128)(2,1)}, bf16[3072,256]{1,0:T(8,128)(2,1)}, u32[]{:S(2)}, u32[]{:S(2)}) collective-permute-start(bf16[3072,256]{1,0:T(8,128)(2,1)} %shard_map.116), channel_id=1, source_target_pairs={{0,16},{1,17},{2,18},{3,19},{4,20},{5,21},{6,22},{7,23},{8,24},{9,... | collective-permute-start | bytes 4718600 | tf_op jit(solution)/shard_map/ppermute | solution.py:333
  23.1 72.7 %collective-permute-start.16 = (bf16[3072,256]{1,0:T(8,128)(2,1)}, bf16[3072,256]{1,0:T(8,128)(2,1)}, u32[]{:S(2)}, u32[]{:S(2)}) collective-permute-start(bf16[3072,256]{1,0:T(8,128)(2,1)} %shard_map.114), channel_id=1, source_target_pairs={{8,24},{9,25},{10,26},{11,27},{12,28},{13,29},{14,30},{15,31},{24,... | collective-permute-start | bytes 4718600 | tf_op jit(solution)/shard_map/ppermute | solution.py:333
  51.1 26.8 %collective-permute-start.10 = (bf16[64,1024]{1,0:T(8,128)(2,1)S(1)}, bf16[64,1024]{1,0:T(8,128)(2,1)S(1)}, u32[]{:S(2)}, u32[]{:S(2)}) collective-permute-start(bf16[64,1024]{1,0:T(8,128)(2,1)S(1)} %get-tuple-element.46), channel_id=1, source_target_pairs={{4,26},{6,24},{20,10},{22,8}} | collective-permute-start | bytes 393224 | tf_op jit(solution)/shard_map/ppermute | solution.py:333
  52.4 26.8 %collective-permute-start.7 = (bf16[64,1024]{1,0:T(8,128)(2,1)S(1)}, bf16[64,1024]{1,0:T(8,128)(2,1)S(1)}, u32[]{:S(2)}, u32[]{:S(2)}) collective-permute-start(bf16[64,1024]{1,0:T(8,128)(2,1)S(1)} %get-tuple-element.45), channel_id=1, source_target_pairs={{4,8},{6,10},{20,24},{22,26}} | collective-permute-start | bytes 393224 | tf_op jit(solution)/shard_map/ppermute | solution.py:333
  53.7 25.8 %collective-permute-start.8 = (bf16[64,1024]{1,0:T(8,128)(2,1)S(1)}, bf16[64,1024]{1,0:T(8,128)(2,1)S(1)}, u32[]{:S(2)}, u32[]{:S(2)}) collective-permute-start(bf16[64,1024]{1,0:T(8,128)(2,1)S(1)} %get-tuple-element.45), channel_id=1, source_target_pairs={{4,10},{6,8},{20,26},{22,24}} | collective-permute-start | bytes 393224 | tf_op jit(solution)/shard_map/ppermute | solution.py:333
  77.9 7.2 %collective-permute-start.9 = (bf16[64,1024]{1,0:T(8,128)(2,1)S(1)}, bf16[64,1024]{1,0:T(8,128)(2,1)S(1)}, u32[]{:S(2)}, u32[]{:S(2)}) collective-permute-start(bf16[64,1024]{1,0:T(8,128)(2,1)S(1)} %get-tuple-element.46), channel_id=1, source_target_pairs={{4,24},{6,26},{20,8},{22,10}} | collective-permute-start | bytes 393224 | tf_op jit(solution)/shard_map/ppermute | solution.py:333
  85.1 65.7 %collective-permute-start.26 = (bf16[3072,256]{1,0:T(8,128)(2,1)}, bf16[3072,256]{1,0:T(8,128)(2,1)}, u32[]{:S(2)}, u32[]{:S(2)}) collective-permute-start(bf16[3072,256]{1,0:T(8,128)(2,1)} %shard_map.114), channel_id=1, source_target_pairs={{0,16},{1,17},{2,18},{3,19},{4,20},{5,21},{6,22},{7,23},{16,0},{17... | collective-permute-start | bytes 4718600 | tf_op jit(solution)/shard_map/ppermute | solution.py:333
  104.1 22.9 %collective-permute-start.18 = (bf16[64,1024]{1,0:T(8,128)(2,1)}, bf16[64,1024]{1,0:T(8,128)(2,1)S(1)}, u32[]{:S(2)}, u32[]{:S(2)}) collective-permute-start(bf16[64,1024]{1,0:T(8,128)(2,1)} %get-tuple-element.63), channel_id=1, source_target_pairs={{13,8},{15,10},{29,24},{31,26}} | collective-permute-start | bytes 393224 | tf_op jit(solution)/shard_map/ppermute | solution.py:333
  105.4 24.9 %collective-permute-start.19 = (bf16[64,1024]{1,0:T(8,128)(2,1)}, bf16[64,1024]{1,0:T(8,128)(2,1)S(1)}, u32[]{:S(2)}, u32[]{:S(2)}) collective-permute-start(bf16[64,1024]{1,0:T(8,128)(2,1)} %get-tuple-element.63), channel_id=1, source_target_pairs={{13,10},{15,8},{29,26},{31,24}} | collective-permute-start | bytes 393224 | tf_op jit(solution)/shard_map/ppermute | solution.py:333
  106.7 25.3 %collective-permute-start.20 = (bf16[64,1024]{1,0:T(8,128)(2,1)}, bf16[64,1024]{1,0:T(8,128)(2,1)}, u32[]{:S(2)}, u32[]{:S(2)}) collective-permute-start(bf16[64,1024]{1,0:T(8,128)(2,1)} %get-tuple-element.64), channel_id=1, source_target_pairs={{13,24},{15,26},{29,8},{31,10}} | collective-permute-start | bytes 393224 | tf_op jit(solution)/shard_map/ppermute | solution.py:333
  108.0 26.4 %collective-permute-start.21 = (bf16[64,1024]{1,0:T(8,128)(2,1)}, bf16[64,1024]{1,0:T(8,128)(2,1)}, u32[]{:S(2)}, u32[]{:S(2)}) collective-permute-start(bf16[64,1024]{1,0:T(8,128)(2,1)} %get-tuple-element.64), channel_id=1, source_target_pairs={{13,26},{15,24},{29,10},{31,8}} | collective-permute-start | bytes 393224 | tf_op jit(solution)/shard_map/ppermute | solution.py:333
  143.0 6.7 %collective-permute-start.22 = (bf16[64,1024]{1,0:T(8,128)(2,1)S(1)}, bf16[64,1024]{1,0:T(8,128)(2,1)S(1)}, u32[]{:S(2)}, u32[]{:S(2)}) collective-permute-start(bf16[64,1024]{1,0:T(8,128)(2,1)S(1)} %get-tuple-element.66), channel_id=1, source_target_pairs={{8,4},{10,6},{24,20},{26,22}} | collective-permute-start | bytes 393224 | tf_op jit(solution)/shard_map/ppermute | solution.py:333
  144.3 5.4 %collective-permute-start.23 = (bf16[64,1024]{1,0:T(8,128)(2,1)S(1)}, bf16[64,1024]{1,0:T(8,128)(2,1)S(1)}, u32[]{:S(2)}, u32[]{:S(2)}) collective-permute-start(bf16[64,1024]{1,0:T(8,128)(2,1)S(1)} %get-tuple-element.66), channel_id=1, source_target_pairs={{8,6},{10,4},{24,22},{26,20}} | collective-permute-start | bytes 393224 | tf_op jit(solution)/shard_map/ppermute | solution.py:333
  151.6 5.7 %collective-permute-start.28 = (bf16[64,1024]{1,0:T(8,128)(2,1)S(1)}, bf16[64,1024]{1,0:T(8,128)(2,1)S(1)}, u32[]{:S(2)}, u32[]{:S(2)}) collective-permute-start(bf16[64,1024]{1,0:T(8,128)(2,1)S(1)} %get-tuple-element.75), channel_id=1, source_target_pairs={{4,1},{6,3},{20,17},{22,19}} | collective-permute-start | bytes 393224 | tf_op jit(solution)/shard_map/ppermute | solution.py:333
  154.4 8.0 %collective-permute-start.27 = (bf16[256,1024]{1,0:T(8,128)(2,1)S(1)}, bf16[256,1024]{1,0:T(8,128)(2,1)S(1)}, u32[]{:S(2)}, u32[]{:S(2)}) collective-permute-start(bf16[256,1024]{1,0:T(8,128)(2,1)S(1)} %slice.113), channel_id=1, source_target_pairs={{1,0},{3,2},{4,5},{6,7},{8,9},{10,11},{13,12},{15,14},{17,16},{19,... | collective-permute-start | bytes 1572872 | tf_op jit(solution)/shard_map/ppermute | solution.py:333
  158.4 48.3 %collective-permute-start.37 = (bf16[128,1024]{1,0:T(8,128)(2,1)S(1)}, bf16[128,1024]{1,0:T(8,128)(2,1)S(1)}, u32[]{:S(2)}, u32[]{:S(2)}) collective-permute-start(bf16[128,1024]{1,0:T(8,128)(2,1)S(1)} %broadcast_select_fusion.3), channel_id=1, source_target_pairs={{0,16},{1,17},{2,18},{3,19},{16,0},{17,1},{18,2},{19,3}} | collective-permute-start | bytes 786440 | tf_op jit(solution)/shard_map/ppermute | solution.py:333
  166.3 40.5 %collective-permute-start.36 = (bf16[128,384]{1,0:T(8,128)(2,1)S(1)}, bf16[128,384]{1,0:T(8,128)(2,1)S(1)}, u32[]{:S(2)}, u32[]{:S(2)}) collective-permute-start(bf16[128,384]{1,0:T(8,128)(2,1)S(1)} %constant_dynamic-slice_fusion), channel_id=1, source_target_pairs={{0,16},{1,17},{2,18},{3,19},{4,20},{5,21},{6,22},{7,23},{8,24},{9,... | collective-permute-start | bytes 294920 | tf_op jit(solution)/shard_map/ppermute | solution.py:333
  187.0 18.7 %collective-permute-start.35 = (bf16[128,768]{1,0:T(8,128)(2,1)S(1)}, bf16[128,768]{1,0:T(8,128)(2,1)S(1)}, u32[]{:S(2)}, u32[]{:S(2)}) collective-permute-start(bf16[128,768]{1,0:T(8,128)(2,1)S(1)} %fusion.27), channel_id=1, source_target_pairs={{4,20},{5,21},{6,22},{7,23},{8,24},{9,25},{10,26},{11,27},{12,28},... | collective-permute-start | bytes 589832 | tf_op jit(solution)/shard_map/ppermute | solution.py:333
  191.8 13.9 %collective-permute-start.34 = (bf16[128,768]{1,0:T(8,128)(2,1)S(1)}, bf16[128,768]{1,0:T(8,128)(2,1)S(1)}, u32[]{:S(2)}, u32[]{:S(2)}) collective-permute-start(bf16[128,768]{1,0:T(8,128)(2,1)S(1)} %fusion.26), channel_id=1, source_target_pairs={{0,16},{1,17},{2,18},{3,19},{16,0},{17,1},{18,2},{19,3}} | collective-permute-start | bytes 589832 | tf_op jit(solution)/shard_map/ppermute | solution.py:333
  192.5 6.1 %collective-permute-start.33 = (bf16[128,512]{1,0:T(8,128)(2,1)S(1)}, bf16[128,512]{1,0:T(8,128)(2,1)S(1)}, u32[]{:S(2)}, u32[]{:S(2)}) collective-permute-start(bf16[128,512]{1,0:T(8,128)(2,1)S(1)} %constant_dynamic-slice_fusion.1), channel_id=1, source_target_pairs={{0,16},{1,17},{2,18},{3,19},{4,20},{5,21},{6,22},{7,23},{8,24},{9,... | collective-permute-start | bytes 393224 | tf_op jit(solution)/shard_map/ppermute | solution.py:333
  198.6 15.1 %collective-permute-start.38 = (bf16[128,1024]{1,0:T(8,128)(2,1)S(1)}, bf16[128,1024]{1,0:T(8,128)(2,1)S(1)}, u32[]{:S(2)}, u32[]{:S(2)}) collective-permute-start(bf16[128,1024]{1,0:T(8,128)(2,1)S(1)} %slice.91), channel_id=1, source_target_pairs={{4,20},{5,21},{6,22},{7,23},{8,24},{9,25},{10,26},{11,27},{12,28},... | collective-permute-start | bytes 786440 | tf_op jit(solution)/shard_map/ppermute | solution.py:333
  (33 other events, 120.2 us)

commit v3 on v2

--- a/solution.py
+++ b/solution.py
@@ -18,11 +18,6 @@
 contract_last = (((1,), (1,)), ((), ()))
 
 
-def norm_scale(rows):
-    wide = rows.astype(jnp.float32)
-    return lax.rsqrt(jnp.mean(wide * wide, axis=1, keepdims=True) + epsilon)
-
-
 def dot(left, right, dims=(((1,), (0,)), ((), ()))):
     return lax.dot_general(left, right, dims, preferred_element_type=jnp.float32)
 
@@ -31,11 +26,6 @@
     new_moment = momentum_decay * moment + delta
     new_weight = weight - outer_rate * (momentum_decay * new_moment + delta)
     return new_weight.astype(jnp.bfloat16), new_moment.astype(jnp.bfloat16)
-
-
-def slope_of(preact):
-    gate = jax.nn.sigmoid(preact)
-    return gate * (1.0 + preact * (1.0 - gate))
 
 
 def from_panels(array, rows):
@@ -291,6 +281,68 @@
     return list(results[:count]), results[count]
 
 
+def share_kernel(sz, whole, *refs):
+    if whole:
+        known, payload, normed_ref, hidden_ref, slope, weights, sem = refs
+    else:
+        known, slope, payload, grad_pre, weights, sem = refs
+    panel, width, hidden_size = sz.panel, sz.width, sz.local_hidden
+    rows_count = sz.row_count
+    which = 0 if whole else 1
+    copy = pltpu.make_async_copy(payload.at[pl.ds(which * sz.half, sz.half)], weights, sem)
+    copy.start()
+    if whole:
+        wide = known[...].astype(jnp.float32)
+        inverse_rms = lax.rsqrt(jnp.mean(wide * wide, axis=1, keepdims=True) + epsilon)
+        normed = (wide * inverse_rms).astype(jnp.bfloat16)
+        normed_ref[...] = normed
+        copy.wait()
+        for p in range(sz.panels_in):
+            preact = dot(normed, weights[p * width : (p + 1) * width, :]) * sz.scale_in
+            gate = jax.nn.sigmoid(preact)
+            here = slice(p * panel, (p + 1) * panel)
+            hidden_ref[:, here] = (preact * gate).astype(jnp.bfloat16)
+            slope[:, here] = gate * (1.0 + preact * (1.0 - gate))
+    else:
+        copy.wait()
+        grad_hidden = jnp.zeros((rows_count, hidden_size), jnp.float32)
+        for n in range(sz.panels_out):
+            piece = known[:, n * panel : (n + 1) * panel]
+            weight = weights[n * hidden_size : (n + 1) * hidden_size, :]
+            grad_hidden = grad_hidden + dot(piece, weight, contract_last)
+        grad_pre[...] = (grad_hidden * sz.scale_out * slope[...]).astype(jnp.bfloat16)
+
+
+def share_call(sz, operands, payload):
+    whole = len(operands) == 1
+    rows_count, hidden_size = sz.row_count, sz.local_hidden
+    narrow = jax.ShapeDtypeStruct((rows_count, hidden_size), jnp.bfloat16)
+    shapes = [narrow]
+    if whole:
+        shapes = [
+            jax.ShapeDtypeStruct((rows_count, sz.width), jnp.bfloat16),
+            narrow,
+            jax.ShapeDtypeStruct((rows_count, hidden_size), jnp.float32),
+        ]
+    inside = pl.BlockSpec(memory_space=pltpu.VMEM)
+    return pl.pallas_call(
+        functools.partial(share_kernel, sz, whole),
+        out_shape=shapes,
+        in_specs=[inside] * len(operands) + [pl.BlockSpec(memory_space=pl.ANY)],
+        out_specs=[inside] * len(shapes),
+        scratch_shapes=[
+            pltpu.VMEM((sz.half, sz.panel), jnp.bfloat16),
+            pltpu.SemaphoreType.DMA,
+        ],
+        compiler_params=pltpu.CompilerParams(vmem_limit_bytes=24 * 1024 * 1024),
+        cost_estimate=pl.CostEstimate(
+            flops=2 * rows_count * sz.width * hidden_size,
+            bytes_accessed=2 * sz.half * sz.panel,
+            transcendentals=0,
+        ),
+    )(*operands, payload)
+
+
 def per_device(inputs, targets, weight_a, weight_b, moment_a, moment_b, routes, partners):
     replicas = lax.axis_size("replica")
     sections = lax.axis_size("section")
@@ -399,6 +451,9 @@
     early = range(sections // 2, sections)
     late = range(sections // 2)
     far_states_in = exchange(packed_in, every)
+    payloads, edges, far_states_in, packed_out = lax.optimization_barrier(
+        (payloads, edges, far_states_in, packed_out)
+    )
     far_states_out = exchange(packed_out, early)
 
     offsets = jnp.arange(replicas, dtype=jnp.int32)
@@ -441,6 +496,19 @@
         return [one.reshape(row_count, width) for one in moved]
 
     state = jnp.zeros((5 * row_count, 2 * local_hidden), jnp.float32)
+
+    def part_of(state, k):
+        return state[k * row_count : (k + 1) * row_count, :width].astype(jnp.bfloat16)
+
+    row_parts = []
+
+    def spread_rows(received, state, active):
+        received, rows, row_parts[:] = lax.optimization_barrier(
+            (received, part_of(state, 0), row_parts)
+        )
+        row_parts.append(from_holders(rows, 1, active))
+        return received
+
     received = []
     for step in every:
         sends, state = chain_step(
@@ -450,41 +518,38 @@
             received = send_blocks(sends, back, slots[step], step, 1)
         else:
             received = [sends[0], from_holders(sends[0], 2, [links])]
+        if len(late) - 1 <= step < links:
+            received = spread_rows(received, state, late if step < len(late) else [step])
         if step == len(late) - 1:
             received, packed_out = lax.optimization_barrier((received, packed_out))
             far_late = exchange(packed_out, late)
         if step == len(late):
-            received, far_states_in, far_states_out = lax.optimization_barrier(
-                (received, far_states_in, far_states_out)
-            )
+            received, far_states_out = lax.optimization_barrier((received, far_states_out))
 
     for step in reversed(range(1, sections)):
         sends, state = chain_step(
             sz, step, False, table, received, edges if step == links else [], payloads, state
         )
         received = send_blocks(sends, slots[step - 1], back, step, -1)
+        if step == links:
+            received = spread_rows(received, state, [links])
         if step == len(late):
-            received, far_late = lax.optimization_barrier((received, far_late))
-
-    known = state[: 2 * row_count, :width].astype(jnp.bfloat16)
-    known = jnp.where(is_holder, known, from_holders(known, 1, every))
-    own_rows, upstream = known[:row_count], known[row_count:]
-    inverse_rms = norm_scale(own_rows)
-    normed = (own_rows.astype(jnp.float32) * inverse_rms).astype(jnp.bfloat16)
-    preact = dot(normed, weight_in) * scale_in
-    hidden = jax.nn.silu(preact).astype(jnp.bfloat16)
-    slope = slope_of(preact)
-
-    def before_slope(upstream):
-        grad_hidden = dot(upstream, weight_out, contract_last) * scale_out
-        return (grad_hidden * slope).astype(jnp.bfloat16)
-
-    grad_pre = before_slope(upstream)
-    far_normed = exchange([piece(normed, pieces_in[e], size_in, 1) for e in others], every)
-    far_hidden = exchange([piece(hidden, pieces_out[e], size_out, 1) for e in others], every)
-    rest = range(1, sections)
-    far_up = exchange([upstream] * len(others), rest)
-    far_pre = exchange([grad_pre] * len(others), rest)
+            received, far_late, row_parts = lax.optimization_barrier(
+                (received, far_late, row_parts)
+            )
+
+    own_rows = jnp.where(is_holder, part_of(state, 0), sum(row_parts[1:], row_parts[0]))
+    normed, hidden, slope = share_call(sz, [own_rows], payload)
+
+    def bundle(e):
+        first, second = normed, hidden
+        first = piece(first, pieces_in[e], size_in, 1)
+        return jnp.concatenate([first, piece(second, pieces_out[e], size_out, 1)], axis=1)
+
+    bundles = exchange([bundle(e) for e in others], every)
+    received, bundles = lax.optimization_barrier((received, bundles))
+    far_normed = [one[:, :size_in] for one in bundles]
+    far_hidden = [one[:, size_in:] for one in bundles]
 
     halves = []
     for a in range(2):
@@ -497,21 +562,11 @@
                 )
         halves.append(half.astype(jnp.float32))
     first_up = (halves[0] + halves[1]).astype(jnp.bfloat16)
-    first_up = jnp.where(is_holder, first_up, from_holders(first_up, 1, [0]))
-    first_pre = before_slope(first_up)
-    here = section_id == 0
-
-    def merge(first, other):
-        return jnp.where(here, first, other)
-
-    far_up = [
-        merge(one, two) for one, two in zip(exchange([first_up] * len(others), [0]), far_up)
-    ]
-    far_pre = [
-        merge(one, two) for one, two in zip(exchange([first_pre] * len(others), [0]), far_pre)
-    ]
-    upstream = merge(first_up, upstream)
-    grad_pre = merge(first_pre, grad_pre)
+    upstream = jnp.where(section_id == 0, first_up, part_of(state, 1))
+    upstream = jnp.where(is_holder, upstream, from_holders(upstream, 1, every))
+    far_up = exchange([upstream] * len(others), every)
+    (grad_pre,) = share_call(sz, [upstream, slope], payload)
+    far_pre = exchange([grad_pre] * len(others), every)
     far_states_out = [
         jnp.where(section_id < len(late), one, two)
         for one, two in zip(far_late, far_states_out)

time: 217 us -> 203 us (0.935)
  the two profiles are of different devices: /device:TPU:4 before, /device:TPU:0 now
where the time goes in v3:
time: 203 us; the launch traced here: 202 us
  waiting for transfers between devices  111 us (55%)
  starting transfers between devices  43.3 us (21%)
  local copies, waits for them, and re-layouts  20.4 us (10%)
  Pallas kernels  12.9 us (6%)
  other arithmetic  5.54 us (3%)
  matrix products  5.33 us (3%)
  between operations  4.09 us (2%)
    ppermute x38, waiting for transfers between devices, move(): return lax.ppermute(array, axes, pairs)  111 us
    ppermute x38, starting transfers between devices, move(): return lax.ppermute(array, axes, pairs)  43.3 us
    unnamed x40, local copies, waits for them, and re-layouts  16.5 us
    pallas_call x3, Pallas kernels, pack(): pl.pallas_call(functools.partial(pack_kernel, heights, panel), out_shape=...  5.97 us
    pallas_call x7, Pallas kernels, chain_step(): pl.pallas_call(functools.partial(chain_kernel, sz, step, forward, (len(re...  5.46 us
    dot_general x6, matrix products, dot(): lax.dot_general(left, right, dims, preferred_element_type=jnp.float32)  5.33 us
  transfers between devices with their start and end apart: 38, of which 6 were waited for; matrix products, arithmetic and copies ran while one was open for 5% of the time, Pallas kernels for 5%

profile of v3, /device:TPU:0, one launch (start us, length us, event | category | flops | bytes accessed | tf_op | source)
XLA Modules:
  0.0 202.4 jit_solution(4030738760830840937)
XLA Ops:
  1.5 1.4 copy-done.3
  2.9 1.4 copy-done.6
  4.3 2.0 %shard_map.111.refs_3_.refs_5_.refs_1_.refs_2_ = bf16[6272,256]{1,0:T(8,128)(2,1)S(1)} custom-call(s32[1,3]{1,0:T(1,128)S(1)} %broadcast_25_starts.2.starts, bf16[1024,768]{1,0:T(8,128)(2,1)S(1)} %bitcast.68, bf16[768,1024]{1,0:T(8,128)(2,1)S(1)} %bitcast.70, bf16[128,256]{1,0:T(8,128)(2,1)S(1)} %select_bitcast_fusion.refs_2_), custom_call_target="tpu_custom_call" | custom-call | bytes 6422528 | tf_op jit(solution)/shard_map/pallas_call | solution.py:67
  6.4 6.6 %collective-permute-start = (bf16[6272,256]{1,0:T(8,128)(2,1)S(1)}, bf16[6272,256]{1,0:T(8,128)(2,1)}, u32[]{:S(2)}, u32[]{:S(2)}) collective-permute-start(bf16[6272,256]{1,0:T(8,128)(2,1)S(1)} %shard_map.111.refs_3_.refs_5_.refs_1_.refs_2_), channel_id=1, source_target_pairs={{0,1},{2,3},{5,4},{7,6},{9,8},{11,10},{12,13},{14,15},{16,17},{18,... | collective-permute-start | bytes 9633800 | tf_op jit(solution)/shard_map/ppermute | solution.py:385
  16.0 1.4 copy-done.9
  17.4 1.9 shard_map.112
  19.3 1.6 collective-permute-start.3
  21.5 3.2 %collective-permute-start.2 = (bf16[128,256]{1,0:T(8,128)(2,1)S(1)}, bf16[128,256]{1,0:T(8,128)(2,1)S(1)}, u32[]{:S(2)}, u32[]{:S(2)}) collective-permute-start(bf16[128,256]{1,0:T(8,128)(2,1)S(1)} %select_bitcast_fusion.refs_2_), channel_id=1, source_target_pairs={{2,1},{0,3},{14,13},{12,15},{18,17},{16,19},{30,29},{28,31}} | collective-permute-start | bytes 196616 | tf_op jit(solution)/shard_map/ppermute | solution.py:385
  27.7 1.4 copy-done.11
  29.1 2.0 %shard_map.113 = bf16[3072,256]{1,0:T(8,128)(2,1)} custom-call(s32[1,2]{1,0:T(1,128)S(1)} %broadcast_in_dim.35.starts, bf16[768,1024]{1,0:T(8,128)(2,1)S(1)} %bitcast.71, bf16[768,1024]{1,0:T(8,128)(2,1)S(1)} %bitcast.73), custom_call_target="tpu_custom_call" | custom-call | bytes 3145728 | tf_op jit(solution)/shard_map/pallas_call | solution.py:67
  31.2 16.3 %collective-permute-done.2.refs_2_.refs_4_ = bf16[128,256]{1,0:T(8,128)(2,1)S(1)} collective-permute-done((bf16[128,256]{1,0:T(8,128)(2,1)S(1)}, bf16[128,256]{1,0:T(8,128)(2,1)S(1)}, u32[]{:S(2)}, u32[]{:S(2)}) %collective-permute-start.2) | collective-permute-done | bytes 65568 | tf_op jit(solution)/shard_map/ppermute | solution.py:385
  47.5 4.2 %collective-permute-done.3 = bf16[3072,256]{1,0:T(8,128)(2,1)} collective-permute-done((bf16[3072,256]{1,0:T(8,128)(2,1)}, bf16[3072,256]{1,0:T(8,128)(2,1)}, u32[]{:S(2)}, u32[]{:S(2)}) %collective-permute-start.3) | collective-permute-done | bytes 1572896 | tf_op jit(solution)/shard_map/ppermute | solution.py:385
  51.7 1.8 collective-permute-start.17
  61.1 3.6 %collective-permute-start.28 = (bf16[3072,256]{1,0:T(8,128)(2,1)}, bf16[3072,256]{1,0:T(8,128)(2,1)}, u32[]{:S(2)}, u32[]{:S(2)}) collective-permute-start(bf16[3072,256]{1,0:T(8,128)(2,1)} %shard_map.113), channel_id=1, source_target_pairs={{0,16},{1,17},{2,18},{3,19},{4,20},{5,21},{6,22},{7,23},{16,0},{17... | collective-permute-start | bytes 4718600 | tf_op jit(solution)/shard_map/ppermute | solution.py:385
  69.6 16.5 %collective-permute-done.16 = bf16[128,1024]{1,0:T(8,128)(2,1)S(1)} collective-permute-done((bf16[128,1024]{1,0:T(8,128)(2,1)S(1)}, bf16[128,1024]{1,0:T(8,128)(2,1)S(1)}, u32[]{:S(2)}, u32[]{:S(2)}) %collective-permute-start.16) | collective-permute-done | bytes 262176 | tf_op jit(solution)/shard_map/ppermute | solution.py:385
  89.9 1.9 copy-done.1
  98.7 2.1 %copy-done.2 = f32[640,1536]{1,0:T(8,128)S(1)} copy-done((f32[640,1536]{1,0:T(8,128)S(1)}, f32[640,1536]{1,0:T(8,128)}, u32[]{:S(2)}) %copy-start.2) | copy-done | bytes 3932184
  104.9 1.5 fusion.37
  113.4 1.6 broadcast_select_fusion
  115.1 3.7 %collective-permute-done.34 = bf16[128,896]{1,0:T(8,128)(2,1)S(1)} collective-permute-done((bf16[128,896]{1,0:T(8,128)(2,1)S(1)}, bf16[128,896]{1,0:T(8,128)(2,1)S(1)}, u32[]{:S(2)}, u32[]{:S(2)}) %collective-permute-start.34) | collective-permute-done | bytes 229408 | tf_op jit(solution)/shard_map/ppermute | solution.py:385
  119.0 1.5 collective-permute-start.35
  120.7 62.2 %collective-permute-done.35 = bf16[128,1024]{1,0:T(8,128)(2,1)S(1)} collective-permute-done((bf16[128,1024]{1,0:T(8,128)(2,1)S(1)}, bf16[128,1024]{1,0:T(8,128)(2,1)S(1)}, u32[]{:S(2)}, u32[]{:S(2)}) %collective-permute-start.35) | collective-permute-done | bytes 262176 | tf_op jit(solution)/shard_map/ppermute | solution.py:385
  188.3 1.6 collective-permute-start.36
  190.2 7.8 %collective-permute-done.36 = bf16[128,768]{1,0:T(8,128)(2,1)S(1)} collective-permute-done((bf16[128,768]{1,0:T(8,128)(2,1)S(1)}, bf16[128,768]{1,0:T(8,128)(2,1)S(1)}, u32[]{:S(2)}, u32[]{:S(2)}) %collective-permute-start.36) | collective-permute-done | bytes 196640 | tf_op jit(solution)/shard_map/ppermute | solution.py:385
  (146 shorter events, 49.1 us)
Async XLA Ops:
  6.4 45.3 %collective-permute-start = (bf16[6272,256]{1,0:T(8,128)(2,1)S(1)}, bf16[6272,256]{1,0:T(8,128)(2,1)}, u32[]{:S(2)}, u32[]{:S(2)}) collective-permute-start(bf16[6272,256]{1,0:T(8,128)(2,1)S(1)} %shard_map.111.refs_3_.refs_5_.refs_1_.refs_2_), channel_id=1, source_target_pairs={{0,1},{2,3},{5,4},{7,6},{9,8},{11,10},{12,13},{14,15},{16,17},{18,... | collective-permute-start | bytes 9633800 | tf_op jit(solution)/shard_map/ppermute | solution.py:385
  19.3 32.4 %collective-permute-start.3 = (bf16[3072,256]{1,0:T(8,128)(2,1)}, bf16[3072,256]{1,0:T(8,128)(2,1)}, u32[]{:S(2)}, u32[]{:S(2)}) collective-permute-start(bf16[3072,256]{1,0:T(8,128)(2,1)} %shard_map.112), channel_id=1, source_target_pairs={{0,16},{1,17},{2,18},{3,19},{4,20},{5,21},{6,22},{7,23},{8,24},{9,... | collective-permute-start | bytes 4718600 | tf_op jit(solution)/shard_map/ppermute | solution.py:385
  20.9 10.4 %collective-permute-start.1 = (bf16[128,256]{1,0:T(8,128)(2,1)S(1)}, bf16[128,256]{1,0:T(8,128)(2,1)S(1)}, u32[]{:S(2)}, u32[]{:S(2)}) collective-permute-start(bf16[128,256]{1,0:T(8,128)(2,1)S(1)} %select_bitcast_fusion.refs_2_), channel_id=1, source_target_pairs={{3,1},{1,3},{15,13},{13,15},{19,17},{17,19},{31,29},{29,31}} | collective-permute-start | bytes 196616 | tf_op jit(solution)/shard_map/ppermute | solution.py:385
  21.5 26.0 %collective-permute-start.2 = (bf16[128,256]{1,0:T(8,128)(2,1)S(1)}, bf16[128,256]{1,0:T(8,128)(2,1)S(1)}, u32[]{:S(2)}, u32[]{:S(2)}) collective-permute-start(bf16[128,256]{1,0:T(8,128)(2,1)S(1)} %select_bitcast_fusion.refs_2_), channel_id=1, source_target_pairs={{2,1},{0,3},{14,13},{12,15},{18,17},{16,19},{30,29},{28,31}} | collective-permute-start | bytes 196616 | tf_op jit(solution)/shard_map/ppermute | solution.py:385
  51.7 34.4 %collective-permute-start.17 = (bf16[3072,256]{1,0:T(8,128)(2,1)}, bf16[3072,256]{1,0:T(8,128)(2,1)}, u32[]{:S(2)}, u32[]{:S(2)}) collective-permute-start(bf16[3072,256]{1,0:T(8,128)(2,1)} %shard_map.113), channel_id=1, source_target_pairs={{8,24},{9,25},{10,26},{11,27},{12,28},{13,29},{14,30},{15,31},{24,... | collective-permute-start | bytes 4718600 | tf_op jit(solution)/shard_map/ppermute | solution.py:385
  61.1 43.1 %collective-permute-start.28 = (bf16[3072,256]{1,0:T(8,128)(2,1)}, bf16[3072,256]{1,0:T(8,128)(2,1)}, u32[]{:S(2)}, u32[]{:S(2)}) collective-permute-start(bf16[3072,256]{1,0:T(8,128)(2,1)} %shard_map.113), channel_id=1, source_target_pairs={{0,16},{1,17},{2,18},{3,19},{4,20},{5,21},{6,22},{7,23},{16,0},{17... | collective-permute-start | bytes 4718600 | tf_op jit(solution)/shard_map/ppermute | solution.py:385
  66.9 19.2 %collective-permute-start.16 = (bf16[128,1024]{1,0:T(8,128)(2,1)S(1)}, bf16[128,1024]{1,0:T(8,128)(2,1)S(1)}, u32[]{:S(2)}, u32[]{:S(2)}) collective-permute-start(bf16[128,1024]{1,0:T(8,128)(2,1)S(1)} %slice.133), channel_id=1, source_target_pairs={{1,0},{3,2},{4,5},{6,7},{17,16},{19,18},{20,21},{22,23}} | collective-permute-start | bytes 786440 | tf_op jit(solution)/shard_map/ppermute | solution.py:385
  87.6 6.8 %collective-permute-start.23 = (bf16[128,1024]{1,0:T(8,128)(2,1)S(1)}, bf16[128,1024]{1,0:T(8,128)(2,1)}, u32[]{:S(2)}, u32[]{:S(2)}) collective-permute-start(bf16[128,1024]{1,0:T(8,128)(2,1)S(1)} %slice.132), channel_id=1, source_target_pairs={{8,9},{10,11},{24,25},{26,27}} | collective-permute-start | bytes 786440 | tf_op jit(solution)/shard_map/ppermute | solution.py:385
  91.7 6.9 %collective-permute-start.19 = (bf16[64,1024]{1,0:T(8,128)(2,1)}, bf16[64,1024]{1,0:T(8,128)(2,1)S(1)}, u32[]{:S(2)}, u32[]{:S(2)}) collective-permute-start(bf16[64,1024]{1,0:T(8,128)(2,1)} %get-tuple-element.111), channel_id=1, source_target_pairs={{13,8},{15,10},{29,24},{31,26}} | collective-permute-start | bytes 393224 | tf_op jit(solution)/shard_map/ppermute | solution.py:385
  92.4 6.2 %collective-permute-start.20 = (bf16[64,1024]{1,0:T(8,128)(2,1)}, bf16[64,1024]{1,0:T(8,128)(2,1)S(1)}, u32[]{:S(2)}, u32[]{:S(2)}) collective-permute-start(bf16[64,1024]{1,0:T(8,128)(2,1)} %get-tuple-element.111), channel_id=1, source_target_pairs={{13,10},{15,8},{29,26},{31,24}} | collective-permute-start | bytes 393224 | tf_op jit(solution)/shard_map/ppermute | solution.py:385
  93.1 5.5 %collective-permute-start.21 = (bf16[64,1024]{1,0:T(8,128)(2,1)}, bf16[64,1024]{1,0:T(8,128)(2,1)}, u32[]{:S(2)}, u32[]{:S(2)}) collective-permute-start(bf16[64,1024]{1,0:T(8,128)(2,1)} %get-tuple-element.112), channel_id=1, source_target_pairs={{13,24},{15,26},{29,8},{31,10}} | collective-permute-start | bytes 393224 | tf_op jit(solution)/shard_map/ppermute | solution.py:385
  94.4 4.2 %collective-permute-start.22 = (bf16[64,1024]{1,0:T(8,128)(2,1)}, bf16[64,1024]{1,0:T(8,128)(2,1)}, u32[]{:S(2)}, u32[]{:S(2)}) collective-permute-start(bf16[64,1024]{1,0:T(8,128)(2,1)} %get-tuple-element.112), channel_id=1, source_target_pairs={{13,26},{15,24},{29,10},{31,8}} | collective-permute-start | bytes 393224 | tf_op jit(solution)/shard_map/ppermute | solution.py:385
  101.5 4.9 %collective-permute-start.24 = (bf16[64,1024]{1,0:T(8,128)(2,1)S(1)}, bf16[64,1024]{1,0:T(8,128)(2,1)S(1)}, u32[]{:S(2)}, u32[]{:S(2)}) collective-permute-start(bf16[64,1024]{1,0:T(8,128)(2,1)S(1)} %get-tuple-element.120), channel_id=1, source_target_pairs={{8,4},{10,6},{24,20},{26,22}} | collective-permute-start | bytes 393224 | tf_op jit(solution)/shard_map/ppermute | solution.py:385
  102.2 4.2 %collective-permute-start.25 = (bf16[64,1024]{1,0:T(8,128)(2,1)S(1)}, bf16[64,1024]{1,0:T(8,128)(2,1)S(1)}, u32[]{:S(2)}, u32[]{:S(2)}) collective-permute-start(bf16[64,1024]{1,0:T(8,128)(2,1)S(1)} %get-tuple-element.120), channel_id=1, source_target_pairs={{8,6},{10,4},{24,22},{26,20}} | collective-permute-start | bytes 393224 | tf_op jit(solution)/shard_map/ppermute | solution.py:385
  102.9 3.5 %collective-permute-start.26 = (bf16[64,1024]{1,0:T(8,128)(2,1)S(1)}, bf16[64,1024]{1,0:T(8,128)(2,1)S(1)}, u32[]{:S(2)}, u32[]{:S(2)}) collective-permute-start(bf16[64,1024]{1,0:T(8,128)(2,1)S(1)} %get-tuple-element.121), channel_id=1, source_target_pairs={{8,20},{10,22},{24,4},{26,6}} | collective-permute-start | bytes 393224 | tf_op jit(solution)/shard_map/ppermute | solution.py:385
  103.6 2.9 %collective-permute-start.27 = (bf16[64,1024]{1,0:T(8,128)(2,1)S(1)}, bf16[64,1024]{1,0:T(8,128)(2,1)S(1)}, u32[]{:S(2)}, u32[]{:S(2)}) collective-permute-start(bf16[64,1024]{1,0:T(8,128)(2,1)S(1)} %get-tuple-element.121), channel_id=1, source_target_pairs={{8,22},{10,20},{24,6},{26,4}} | collective-permute-start | bytes 393224 | tf_op jit(solution)/shard_map/ppermute | solution.py:385
  107.2 7.8 %collective-permute-start.30 = (bf16[64,1024]{1,0:T(8,128)(2,1)S(1)}, bf16[64,1024]{1,0:T(8,128)(2,1)S(1)}, u32[]{:S(2)}, u32[]{:S(2)}) collective-permute-start(bf16[64,1024]{1,0:T(8,128)(2,1)S(1)} %get-tuple-element.136), channel_id=1, source_target_pairs={{4,1},{6,3},{20,17},{22,19}} | collective-permute-start | bytes 393224 | tf_op jit(solution)/shard_map/ppermute | solution.py:385
  107.9 7.1 %collective-permute-start.31 = (bf16[64,1024]{1,0:T(8,128)(2,1)S(1)}, bf16[64,1024]{1,0:T(8,128)(2,1)S(1)}, u32[]{:S(2)}, u32[]{:S(2)}) collective-permute-start(bf16[64,1024]{1,0:T(8,128)(2,1)S(1)} %get-tuple-element.136), channel_id=1, source_target_pairs={{4,3},{6,1},{20,19},{22,17}} | collective-permute-start | bytes 393224 | tf_op jit(solution)/shard_map/ppermute | solution.py:385
  108.6 6.5 %collective-permute-start.32 = (bf16[64,1024]{1,0:T(8,128)(2,1)S(1)}, bf16[64,1024]{1,0:T(8,128)(2,1)S(1)}, u32[]{:S(2)}, u32[]{:S(2)}) collective-permute-start(bf16[64,1024]{1,0:T(8,128)(2,1)S(1)} %get-tuple-element.137), channel_id=1, source_target_pairs={{4,17},{6,19},{20,1},{22,3}} | collective-permute-start | bytes 393224 | tf_op jit(solution)/shard_map/ppermute | solution.py:385
  109.2 5.8 %collective-permute-start.33 = (bf16[64,1024]{1,0:T(8,128)(2,1)S(1)}, bf16[64,1024]{1,0:T(8,128)(2,1)S(1)}, u32[]{:S(2)}, u32[]{:S(2)}) collective-permute-start(bf16[64,1024]{1,0:T(8,128)(2,1)S(1)} %get-tuple-element.137), channel_id=1, source_target_pairs={{4,19},{6,17},{20,3},{22,1}} | collective-permute-start | bytes 393224 | tf_op jit(solution)/shard_map/ppermute | solution.py:385
  112.7 6.1 %collective-permute-start.34 = (bf16[128,896]{1,0:T(8,128)(2,1)S(1)}, bf16[128,896]{1,0:T(8,128)(2,1)S(1)}, u32[]{:S(2)}, u32[]{:S(2)}) collective-permute-start(bf16[128,896]{1,0:T(8,128)(2,1)S(1)} %pad_maximum_fusion.2), channel_id=1, source_target_pairs={{0,16},{1,17},{2,18},{3,19},{4,20},{5,21},{6,22},{7,23},{8,24},{9,... | collective-permute-start | bytes 688136 | tf_op jit(solution)/shard_map/ppermute | solution.py:385
  119.0 63.9 %collective-permute-start.35 = (bf16[128,1024]{1,0:T(8,128)(2,1)S(1)}, bf16[128,1024]{1,0:T(8,128)(2,1)S(1)}, u32[]{:S(2)}, u32[]{:S(2)}) collective-permute-start(bf16[128,1024]{1,0:T(8,128)(2,1)S(1)} %fusion.28), channel_id=1, source_target_pairs={{1,0},{3,2},{4,5},{6,7},{8,9},{10,11},{13,12},{15,14},{17,16},{19,... | collective-permute-start | bytes 786440 | tf_op jit(solution)/shard_map/ppermute | solution.py:385
  184.6 14.5 %collective-permute-start.37 = (bf16[128,1024]{1,0:T(8,128)(2,1)S(1)}, bf16[128,1024]{1,0:T(8,128)(2,1)S(1)}, u32[]{:S(2)}, u32[]{:S(2)}) collective-permute-start(bf16[128,1024]{1,0:T(8,128)(2,1)S(1)} %broadcast_select_fusion.1.refs_0_), channel_id=1, source_target_pairs={{0,16},{1,17},{2,18},{3,19},{4,20},{5,21},{6,22},{7,23},{8,24},{9,... | collective-permute-start | bytes 786440 | tf_op jit(solution)/shard_map/ppermute | solution.py:385
  188.3 9.8 %collective-permute-start.36 = (bf16[128,768]{1,0:T(8,128)(2,1)S(1)}, bf16[128,768]{1,0:T(8,128)(2,1)S(1)}, u32[]{:S(2)}, u32[]{:S(2)}) collective-permute-start(bf16[128,768]{1,0:T(8,128)(2,1)S(1)} %shard_map.122), channel_id=1, source_target_pairs={{0,16},{1,17},{2,18},{3,19},{4,20},{5,21},{6,22},{7,23},{8,24},{9,... | collective-permute-start | bytes 589832 | tf_op jit(solution)/shard_map/ppermute | solution.py:385
  (34 other events, 206.8 us)
